TPU v7x, 128 devices: a whole 4x4x4 slice. The times are simulated.
128 devices in a mesh: row: 16 (over z, x), col: 8 (over y, core).
Axes of the slice: x: 4, y: 4, z: 4, core: 2. Of those that a mesh axis runs over, the one named last changes fastest.
Arguments:
- points: float32 [8, 65536], P(None, ('row', 'col')), may hold values from -5 to 5
- lengthscale: float32 [8], replicated, may hold values from 0.6 to 1.6
- outputscale: float32 [1], replicated, may hold values from 0.5 to 1.5
- noise: float32 [1], replicated, may hold values from 0.1 to 0.6
- solution: float32 [8, 65536], P(None, ('row', 'col')), may hold values from -6 to 6
- residual: float32 [8, 65536], P(None, ('row', 'col')), may hold values from -6 to 6
- direction: float32 [8, 65536], P(None, ('row', 'col')), may hold values from -12 to 12
Outputs:
- new_solution: float32 [8, 65536], P(None, ('row', 'col'))
- new_residual: float32 [8, 65536], P(None, ('row', 'col'))
- new_direction: float32 [8, 65536], P(None, ('row', 'col'))
All inputs are finite; a program needn't handle non-finite values.
Results may differ from a plain program's by a relative error of at most 0.000065.
Values sent between devices are 32-bit elements; how exact they have to be, the bound alone decides.
No kernel may reach another device: no remote copies, remote signals or barrier semaphores. Data moves between devices by JAX's collectives and lax.ppermute only.
A program may use at most 64 MiB of HBM per device.

v0:
```python
import jax
import jax.numpy as jnp
from jax import lax
from jax.sharding import PartitionSpec as P

root_five = 5.0**0.5
per_turn = 8
highest = lax.Precision.HIGHEST


def matern_tiles(left, right, outputscale):
    cross = jnp.einsum(
        "fga,fgb->gab", left, right, precision=highest, preferred_element_type=jnp.float32
    )
    left_sq = jnp.sum(left * left, axis=0)
    right_sq = jnp.sum(right * right, axis=0)
    dist_sq = jnp.maximum(left_sq[:, :, None] + right_sq[:, None, :] - 2.0 * cross, 0.0)
    radius = jnp.sqrt(dist_sq)
    return (
        outputscale
        * (1.0 + root_five * radius + 5.0 / 3.0 * dist_sq)
        * jnp.exp(-root_five * radius)
    )


def shards(points, lengthscale, outputscale, noise, solution, residual, direction):
    scaled = points / lengthscale[:, None]
    every_pts, every_dir = (
        lax.all_gather(scaled, ("row", "col"), axis=1, tiled=True),
        lax.all_gather(direction, ("row", "col"), axis=1, tiled=True),
    )
    feats, width = scaled.shape
    columns = direction.shape[0]
    blocks = lax.axis_size(("row", "col"))
    pts_blocks = every_pts.reshape(feats, blocks, width)
    dir_blocks = every_dir.reshape(columns, blocks, width)
    scale_value = outputscale[0]
    offsets = jnp.arange(per_turn, dtype=jnp.int32)

    def full_turn(step, acc):
        cols = step * per_turn + offsets
        left = jnp.broadcast_to(scaled[:, None, :], (feats, per_turn, width))
        tiles = matern_tiles(left, jnp.take(pts_blocks, cols, axis=1), scale_value)
        dir_right = jnp.take(dir_blocks, cols, axis=1)
        return acc + jnp.einsum(
            "gab,sgb->sa", tiles, dir_right, precision=highest, preferred_element_type=jnp.float32
        )

    product = lax.fori_loop(
        0, blocks // per_turn, full_turn, jnp.zeros((columns, width), jnp.float32)
    )
    image = product + noise[0] * direction
    rr_old, curv = lax.psum(
        (jnp.sum(residual * residual, axis=1), jnp.sum(direction * image, axis=1)), ("row", "col")
    )
    alpha = rr_old / curv
    new_residual = residual - alpha[:, None] * image
    rr_new = lax.psum(jnp.sum(new_residual * new_residual, axis=1), ("row", "col"))
    new_solution = solution + alpha[:, None] * direction
    new_direction = new_residual + (rr_new / rr_old)[:, None] * direction
    return (new_solution, new_residual, new_direction)


def solution(mesh):
    return jax.shard_map(
        shards,
        mesh=mesh,
        in_specs=(
            P(None, ("row", "col")),
            P(),
            P(),
            P(),
            P(None, ("row", "col")),
            P(None, ("row", "col")),
            P(None, ("row", "col")),
        ),
        out_specs=(P(None, ("row", "col")), P(None, ("row", "col")), P(None, ("row", "col"))),
        check_vma=False,
    )
```

profile of v0, /device:TPU:1, one launch (start us, length us, event | category | flops | bytes accessed | tf_op | source)
XLA Modules:
  0.0 706.3 jit_solution(11323638645201885983)
XLA Ops:
  10.0 70.6 %all-gather.5.cloned.1.call-done = f32[8,65536]{1,0:T(8,128)} async-done(((f32[8,512]{1,0:T(8,128)}), f32[8,65536]{1,0:T(8,128)}) %all-gather.5.cloned.1.call-update) | async-done | bytes 2097168 | tf_op jit(solution)/shard_map/all_gather | solution.py:29
  80.7 65.9 %all-gather.3.cloned.1.call-done = f32[8,65536]{1,0:T(8,128)} async-done(((f32[8,512]{1,0:T(8,128)}), f32[8,65536]{1,0:T(8,128)}) %all-gather.3.cloned.1.call-update) | async-done | bytes 2097168 | tf_op jit(solution)/shard_map/all_gather | solution.py:30
  146.6 425.1 %while.16 = (s32[]{:T(128)}, f32[8,512]{1,0:T(8,128)S(1)}, f32[8,128,512]{2,0,1:T(8,128)}, f32[]{:T(128)}, f32[512]{0:T(512)S(1)}, /*index=5*/f32[8,128,512]{2,0...) while((s32[]{:T(128)}, f32[8,512]{1,0:T(8,128)S(1)}, f32[8,128,512]{2,0,1:T(8,128)}, ...), condition=%wide.region_5.7_spmd.clone, body=%wide.region_3.6_spmd.clone.sunk | while | flops 425890912 | bytes 17783080 | solution.py:49
  146.6 2.2 gather_fusion
  148.8 9.8 %fusion.61 = f32[8,512,512]{2,1,0:T(8,128)} fusion(f32[8,8,512]{2,1,0:T(8,128)S(1)} %gather_fusion, f32[8,512]{1,0:T(8,128)} %get-tuple-element.298, pred[8]{0:T(512)(128)(4,1)S(1)} %compare_and_fusion.2), kind=kOutput, calls=%fused_computation.28.clone.1 | convolution fusion | flops 201359360 | bytes 8536072 | tf_op jit(solution)/shard_map/while/body/eval_jaxpr/fga,fgb->gab/dot_general | solution.py:12
  158.8 2.1 gather_fusion.1
  160.9 12.3 %fusion.63 = f32[8,512]{1,0:T(8,128)S(1)} fusion(f32[8,512,512]{2,1,0:T(8,128)} %fusion.61, f32[8,512]{1,0:T(8,128)S(1)} %fusion.62, f32[512]{0:T(512)S(1)} %get-tuple-element.296, f32[]{:T(128)} %get-tuple-element.295, f32[8,8,512]{2,1,0:T(8,128)S(1)} %gather_fusion.1, pred[8]{0:T(512)(128)(4,1)S(1)} %compare_and_fusion.2, ...), kind=kOutput, calls=%fused_computation.27.clone.1 | convolution fusion | flops 224436224 | bytes 8570893 | tf_op jit(solution)/shard_map/while/body/eval_jaxpr/gab,sgb->sa/dot_general | solution.py:45
  173.2 2.1 gather_fusion
  175.4 9.8 %fusion.61 = f32[8,512,512]{2,1,0:T(8,128)} fusion(f32[8,8,512]{2,1,0:T(8,128)S(1)} %gather_fusion, f32[8,512]{1,0:T(8,128)} %get-tuple-element.298, pred[8]{0:T(512)(128)(4,1)S(1)} %compare_and_fusion.2), kind=kOutput, calls=%fused_computation.28.clone.1 | convolution fusion | flops 201359360 | bytes 8536072 | tf_op jit(solution)/shard_map/while/body/eval_jaxpr/fga,fgb->gab/dot_general | solution.py:12
  187.5 12.3 %fusion.63 = f32[8,512]{1,0:T(8,128)S(1)} fusion(f32[8,512,512]{2,1,0:T(8,128)} %fusion.61, f32[8,512]{1,0:T(8,128)S(1)} %fusion.62, f32[512]{0:T(512)S(1)} %get-tuple-element.296, f32[]{:T(128)} %get-tuple-element.295, f32[8,8,512]{2,1,0:T(8,128)S(1)} %gather_fusion.1, pred[8]{0:T(512)(128)(4,1)S(1)} %compare_and_fusion.2, ...), kind=kOutput, calls=%fused_computation.27.clone.1 | convolution fusion | flops 224436224 | bytes 8570893 | tf_op jit(solution)/shard_map/while/body/eval_jaxpr/gab,sgb->sa/dot_general | solution.py:45
  202.0 9.8 %fusion.61 = f32[8,512,512]{2,1,0:T(8,128)} fusion(f32[8,8,512]{2,1,0:T(8,128)S(1)} %gather_fusion, f32[8,512]{1,0:T(8,128)} %get-tuple-element.298, pred[8]{0:T(512)(128)(4,1)S(1)} %compare_and_fusion.2), kind=kOutput, calls=%fused_computation.28.clone.1 | convolution fusion | flops 201359360 | bytes 8536072 | tf_op jit(solution)/shard_map/while/body/eval_jaxpr/fga,fgb->gab/dot_general | solution.py:12
  214.1 12.3 %fusion.63 = f32[8,512]{1,0:T(8,128)S(1)} fusion(f32[8,512,512]{2,1,0:T(8,128)} %fusion.61, f32[8,512]{1,0:T(8,128)S(1)} %fusion.62, f32[512]{0:T(512)S(1)} %get-tuple-element.296, f32[]{:T(128)} %get-tuple-element.295, f32[8,8,512]{2,1,0:T(8,128)S(1)} %gather_fusion.1, pred[8]{0:T(512)(128)(4,1)S(1)} %compare_and_fusion.2, ...), kind=kOutput, calls=%fused_computation.27.clone.1 | convolution fusion | flops 224436224 | bytes 8570893 | tf_op jit(solution)/shard_map/while/body/eval_jaxpr/gab,sgb->sa/dot_general | solution.py:45
  228.5 9.8 %fusion.61 = f32[8,512,512]{2,1,0:T(8,128)} fusion(f32[8,8,512]{2,1,0:T(8,128)S(1)} %gather_fusion, f32[8,512]{1,0:T(8,128)} %get-tuple-element.298, pred[8]{0:T(512)(128)(4,1)S(1)} %compare_and_fusion.2), kind=kOutput, calls=%fused_computation.28.clone.1 | convolution fusion | flops 201359360 | bytes 8536072 | tf_op jit(solution)/shard_map/while/body/eval_jaxpr/fga,fgb->gab/dot_general | solution.py:12
  240.6 12.3 %fusion.63 = f32[8,512]{1,0:T(8,128)S(1)} fusion(f32[8,512,512]{2,1,0:T(8,128)} %fusion.61, f32[8,512]{1,0:T(8,128)S(1)} %fusion.62, f32[512]{0:T(512)S(1)} %get-tuple-element.296, f32[]{:T(128)} %get-tuple-element.295, f32[8,8,512]{2,1,0:T(8,128)S(1)} %gather_fusion.1, pred[8]{0:T(512)(128)(4,1)S(1)} %compare_and_fusion.2, ...), kind=kOutput, calls=%fused_computation.27.clone.1 | convolution fusion | flops 224436224 | bytes 8570893 | tf_op jit(solution)/shard_map/while/body/eval_jaxpr/gab,sgb->sa/dot_general | solution.py:45
  255.1 9.8 %fusion.61 = f32[8,512,512]{2,1,0:T(8,128)} fusion(f32[8,8,512]{2,1,0:T(8,128)S(1)} %gather_fusion, f32[8,512]{1,0:T(8,128)} %get-tuple-element.298, pred[8]{0:T(512)(128)(4,1)S(1)} %compare_and_fusion.2), kind=kOutput, calls=%fused_computation.28.clone.1 | convolution fusion | flops 201359360 | bytes 8536072 | tf_op jit(solution)/shard_map/while/body/eval_jaxpr/fga,fgb->gab/dot_general | solution.py:12
  267.2 12.3 %fusion.63 = f32[8,512]{1,0:T(8,128)S(1)} fusion(f32[8,512,512]{2,1,0:T(8,128)} %fusion.61, f32[8,512]{1,0:T(8,128)S(1)} %fusion.62, f32[512]{0:T(512)S(1)} %get-tuple-element.296, f32[]{:T(128)} %get-tuple-element.295, f32[8,8,512]{2,1,0:T(8,128)S(1)} %gather_fusion.1, pred[8]{0:T(512)(128)(4,1)S(1)} %compare_and_fusion.2, ...), kind=kOutput, calls=%fused_computation.27.clone.1 | convolution fusion | flops 224436224 | bytes 8570893 | tf_op jit(solution)/shard_map/while/body/eval_jaxpr/gab,sgb->sa/dot_general | solution.py:45
  281.7 9.8 %fusion.61 = f32[8,512,512]{2,1,0:T(8,128)} fusion(f32[8,8,512]{2,1,0:T(8,128)S(1)} %gather_fusion, f32[8,512]{1,0:T(8,128)} %get-tuple-element.298, pred[8]{0:T(512)(128)(4,1)S(1)} %compare_and_fusion.2), kind=kOutput, calls=%fused_computation.28.clone.1 | convolution fusion | flops 201359360 | bytes 8536072 | tf_op jit(solution)/shard_map/while/body/eval_jaxpr/fga,fgb->gab/dot_general | solution.py:12
  293.8 12.3 %fusion.63 = f32[8,512]{1,0:T(8,128)S(1)} fusion(f32[8,512,512]{2,1,0:T(8,128)} %fusion.61, f32[8,512]{1,0:T(8,128)S(1)} %fusion.62, f32[512]{0:T(512)S(1)} %get-tuple-element.296, f32[]{:T(128)} %get-tuple-element.295, f32[8,8,512]{2,1,0:T(8,128)S(1)} %gather_fusion.1, pred[8]{0:T(512)(128)(4,1)S(1)} %compare_and_fusion.2, ...), kind=kOutput, calls=%fused_computation.27.clone.1 | convolution fusion | flops 224436224 | bytes 8570893 | tf_op jit(solution)/shard_map/while/body/eval_jaxpr/gab,sgb->sa/dot_general | solution.py:45
  306.1 2.1 gather_fusion
  308.2 9.8 %fusion.61 = f32[8,512,512]{2,1,0:T(8,128)} fusion(f32[8,8,512]{2,1,0:T(8,128)S(1)} %gather_fusion, f32[8,512]{1,0:T(8,128)} %get-tuple-element.298, pred[8]{0:T(512)(128)(4,1)S(1)} %compare_and_fusion.2), kind=kOutput, calls=%fused_computation.28.clone.1 | convolution fusion | flops 201359360 | bytes 8536072 | tf_op jit(solution)/shard_map/while/body/eval_jaxpr/fga,fgb->gab/dot_general | solution.py:12
  320.3 12.3 %fusion.63 = f32[8,512]{1,0:T(8,128)S(1)} fusion(f32[8,512,512]{2,1,0:T(8,128)} %fusion.61, f32[8,512]{1,0:T(8,128)S(1)} %fusion.62, f32[512]{0:T(512)S(1)} %get-tuple-element.296, f32[]{:T(128)} %get-tuple-element.295, f32[8,8,512]{2,1,0:T(8,128)S(1)} %gather_fusion.1, pred[8]{0:T(512)(128)(4,1)S(1)} %compare_and_fusion.2, ...), kind=kOutput, calls=%fused_computation.27.clone.1 | convolution fusion | flops 224436224 | bytes 8570893 | tf_op jit(solution)/shard_map/while/body/eval_jaxpr/gab,sgb->sa/dot_general | solution.py:45
  332.6 2.1 gather_fusion
  334.8 9.8 %fusion.61 = f32[8,512,512]{2,1,0:T(8,128)} fusion(f32[8,8,512]{2,1,0:T(8,128)S(1)} %gather_fusion, f32[8,512]{1,0:T(8,128)} %get-tuple-element.298, pred[8]{0:T(512)(128)(4,1)S(1)} %compare_and_fusion.2), kind=kOutput, calls=%fused_computation.28.clone.1 | convolution fusion | flops 201359360 | bytes 8536072 | tf_op jit(solution)/shard_map/while/body/eval_jaxpr/fga,fgb->gab/dot_general | solution.py:12
  346.9 12.3 %fusion.63 = f32[8,512]{1,0:T(8,128)S(1)} fusion(f32[8,512,512]{2,1,0:T(8,128)} %fusion.61, f32[8,512]{1,0:T(8,128)S(1)} %fusion.62, f32[512]{0:T(512)S(1)} %get-tuple-element.296, f32[]{:T(128)} %get-tuple-element.295, f32[8,8,512]{2,1,0:T(8,128)S(1)} %gather_fusion.1, pred[8]{0:T(512)(128)(4,1)S(1)} %compare_and_fusion.2, ...), kind=kOutput, calls=%fused_computation.27.clone.1 | convolution fusion | flops 224436224 | bytes 8570893 | tf_op jit(solution)/shard_map/while/body/eval_jaxpr/gab,sgb->sa/dot_general | solution.py:45
  359.2 2.1 gather_fusion
  361.4 9.8 %fusion.61 = f32[8,512,512]{2,1,0:T(8,128)} fusion(f32[8,8,512]{2,1,0:T(8,128)S(1)} %gather_fusion, f32[8,512]{1,0:T(8,128)} %get-tuple-element.298, pred[8]{0:T(512)(128)(4,1)S(1)} %compare_and_fusion.2), kind=kOutput, calls=%fused_computation.28.clone.1 | convolution fusion | flops 201359360 | bytes 8536072 | tf_op jit(solution)/shard_map/while/body/eval_jaxpr/fga,fgb->gab/dot_general | solution.py:12
  373.5 12.3 %fusion.63 = f32[8,512]{1,0:T(8,128)S(1)} fusion(f32[8,512,512]{2,1,0:T(8,128)} %fusion.61, f32[8,512]{1,0:T(8,128)S(1)} %fusion.62, f32[512]{0:T(512)S(1)} %get-tuple-element.296, f32[]{:T(128)} %get-tuple-element.295, f32[8,8,512]{2,1,0:T(8,128)S(1)} %gather_fusion.1, pred[8]{0:T(512)(128)(4,1)S(1)} %compare_and_fusion.2, ...), kind=kOutput, calls=%fused_computation.27.clone.1 | convolution fusion | flops 224436224 | bytes 8570893 | tf_op jit(solution)/shard_map/while/body/eval_jaxpr/gab,sgb->sa/dot_general | solution.py:45
  385.8 2.1 gather_fusion
  387.9 9.8 %fusion.61 = f32[8,512,512]{2,1,0:T(8,128)} fusion(f32[8,8,512]{2,1,0:T(8,128)S(1)} %gather_fusion, f32[8,512]{1,0:T(8,128)} %get-tuple-element.298, pred[8]{0:T(512)(128)(4,1)S(1)} %compare_and_fusion.2), kind=kOutput, calls=%fused_computation.28.clone.1 | convolution fusion | flops 201359360 | bytes 8536072 | tf_op jit(solution)/shard_map/while/body/eval_jaxpr/fga,fgb->gab/dot_general | solution.py:12
  400.0 12.3 %fusion.63 = f32[8,512]{1,0:T(8,128)S(1)} fusion(f32[8,512,512]{2,1,0:T(8,128)} %fusion.61, f32[8,512]{1,0:T(8,128)S(1)} %fusion.62, f32[512]{0:T(512)S(1)} %get-tuple-element.296, f32[]{:T(128)} %get-tuple-element.295, f32[8,8,512]{2,1,0:T(8,128)S(1)} %gather_fusion.1, pred[8]{0:T(512)(128)(4,1)S(1)} %compare_and_fusion.2, ...), kind=kOutput, calls=%fused_computation.27.clone.1 | convolution fusion | flops 224436224 | bytes 8570893 | tf_op jit(solution)/shard_map/while/body/eval_jaxpr/gab,sgb->sa/dot_general | solution.py:45
  412.3 2.1 gather_fusion
  414.5 9.8 %fusion.61 = f32[8,512,512]{2,1,0:T(8,128)} fusion(f32[8,8,512]{2,1,0:T(8,128)S(1)} %gather_fusion, f32[8,512]{1,0:T(8,128)} %get-tuple-element.298, pred[8]{0:T(512)(128)(4,1)S(1)} %compare_and_fusion.2), kind=kOutput, calls=%fused_computation.28.clone.1 | convolution fusion | flops 201359360 | bytes 8536072 | tf_op jit(solution)/shard_map/while/body/eval_jaxpr/fga,fgb->gab/dot_general | solution.py:12
  424.4 2.1 gather_fusion.1
  426.6 12.3 %fusion.63 = f32[8,512]{1,0:T(8,128)S(1)} fusion(f32[8,512,512]{2,1,0:T(8,128)} %fusion.61, f32[8,512]{1,0:T(8,128)S(1)} %fusion.62, f32[512]{0:T(512)S(1)} %get-tuple-element.296, f32[]{:T(128)} %get-tuple-element.295, f32[8,8,512]{2,1,0:T(8,128)S(1)} %gather_fusion.1, pred[8]{0:T(512)(128)(4,1)S(1)} %compare_and_fusion.2, ...), kind=kOutput, calls=%fused_computation.27.clone.1 | convolution fusion | flops 224436224 | bytes 8570893 | tf_op jit(solution)/shard_map/while/body/eval_jaxpr/gab,sgb->sa/dot_general | solution.py:45
  438.9 2.1 gather_fusion
  441.1 9.8 %fusion.61 = f32[8,512,512]{2,1,0:T(8,128)} fusion(f32[8,8,512]{2,1,0:T(8,128)S(1)} %gather_fusion, f32[8,512]{1,0:T(8,128)} %get-tuple-element.298, pred[8]{0:T(512)(128)(4,1)S(1)} %compare_and_fusion.2), kind=kOutput, calls=%fused_computation.28.clone.1 | convolution fusion | flops 201359360 | bytes 8536072 | tf_op jit(solution)/shard_map/while/body/eval_jaxpr/fga,fgb->gab/dot_general | solution.py:12
  451.0 2.1 gather_fusion.1
  453.2 12.3 %fusion.63 = f32[8,512]{1,0:T(8,128)S(1)} fusion(f32[8,512,512]{2,1,0:T(8,128)} %fusion.61, f32[8,512]{1,0:T(8,128)S(1)} %fusion.62, f32[512]{0:T(512)S(1)} %get-tuple-element.296, f32[]{:T(128)} %get-tuple-element.295, f32[8,8,512]{2,1,0:T(8,128)S(1)} %gather_fusion.1, pred[8]{0:T(512)(128)(4,1)S(1)} %compare_and_fusion.2, ...), kind=kOutput, calls=%fused_computation.27.clone.1 | convolution fusion | flops 224436224 | bytes 8570893 | tf_op jit(solution)/shard_map/while/body/eval_jaxpr/gab,sgb->sa/dot_general | solution.py:45
  467.6 9.8 %fusion.61 = f32[8,512,512]{2,1,0:T(8,128)} fusion(f32[8,8,512]{2,1,0:T(8,128)S(1)} %gather_fusion, f32[8,512]{1,0:T(8,128)} %get-tuple-element.298, pred[8]{0:T(512)(128)(4,1)S(1)} %compare_and_fusion.2), kind=kOutput, calls=%fused_computation.28.clone.1 | convolution fusion | flops 201359360 | bytes 8536072 | tf_op jit(solution)/shard_map/while/body/eval_jaxpr/fga,fgb->gab/dot_general | solution.py:12
  479.7 12.3 %fusion.63 = f32[8,512]{1,0:T(8,128)S(1)} fusion(f32[8,512,512]{2,1,0:T(8,128)} %fusion.61, f32[8,512]{1,0:T(8,128)S(1)} %fusion.62, f32[512]{0:T(512)S(1)} %get-tuple-element.296, f32[]{:T(128)} %get-tuple-element.295, f32[8,8,512]{2,1,0:T(8,128)S(1)} %gather_fusion.1, pred[8]{0:T(512)(128)(4,1)S(1)} %compare_and_fusion.2, ...), kind=kOutput, calls=%fused_computation.27.clone.1 | convolution fusion | flops 224436224 | bytes 8570893 | tf_op jit(solution)/shard_map/while/body/eval_jaxpr/gab,sgb->sa/dot_general | solution.py:45
  494.2 9.8 %fusion.61 = f32[8,512,512]{2,1,0:T(8,128)} fusion(f32[8,8,512]{2,1,0:T(8,128)S(1)} %gather_fusion, f32[8,512]{1,0:T(8,128)} %get-tuple-element.298, pred[8]{0:T(512)(128)(4,1)S(1)} %compare_and_fusion.2), kind=kOutput, calls=%fused_computation.28.clone.1 | convolution fusion | flops 201359360 | bytes 8536072 | tf_op jit(solution)/shard_map/while/body/eval_jaxpr/fga,fgb->gab/dot_general | solution.py:12
  506.3 12.3 %fusion.63 = f32[8,512]{1,0:T(8,128)S(1)} fusion(f32[8,512,512]{2,1,0:T(8,128)} %fusion.61, f32[8,512]{1,0:T(8,128)S(1)} %fusion.62, f32[512]{0:T(512)S(1)} %get-tuple-element.296, f32[]{:T(128)} %get-tuple-element.295, f32[8,8,512]{2,1,0:T(8,128)S(1)} %gather_fusion.1, pred[8]{0:T(512)(128)(4,1)S(1)} %compare_and_fusion.2, ...), kind=kOutput, calls=%fused_computation.27.clone.1 | convolution fusion | flops 224436224 | bytes 8570893 | tf_op jit(solution)/shard_map/while/body/eval_jaxpr/gab,sgb->sa/dot_general | solution.py:45
  520.8 9.8 %fusion.61 = f32[8,512,512]{2,1,0:T(8,128)} fusion(f32[8,8,512]{2,1,0:T(8,128)S(1)} %gather_fusion, f32[8,512]{1,0:T(8,128)} %get-tuple-element.298, pred[8]{0:T(512)(128)(4,1)S(1)} %compare_and_fusion.2), kind=kOutput, calls=%fused_computation.28.clone.1 | convolution fusion | flops 201359360 | bytes 8536072 | tf_op jit(solution)/shard_map/while/body/eval_jaxpr/fga,fgb->gab/dot_general | solution.py:12
  532.9 12.3 %fusion.63 = f32[8,512]{1,0:T(8,128)S(1)} fusion(f32[8,512,512]{2,1,0:T(8,128)} %fusion.61, f32[8,512]{1,0:T(8,128)S(1)} %fusion.62, f32[512]{0:T(512)S(1)} %get-tuple-element.296, f32[]{:T(128)} %get-tuple-element.295, f32[8,8,512]{2,1,0:T(8,128)S(1)} %gather_fusion.1, pred[8]{0:T(512)(128)(4,1)S(1)} %compare_and_fusion.2, ...), kind=kOutput, calls=%fused_computation.27.clone.1 | convolution fusion | flops 224436224 | bytes 8570893 | tf_op jit(solution)/shard_map/while/body/eval_jaxpr/gab,sgb->sa/dot_general | solution.py:45
  547.3 9.8 %fusion.61 = f32[8,512,512]{2,1,0:T(8,128)} fusion(f32[8,8,512]{2,1,0:T(8,128)S(1)} %gather_fusion, f32[8,512]{1,0:T(8,128)} %get-tuple-element.298, pred[8]{0:T(512)(128)(4,1)S(1)} %compare_and_fusion.2), kind=kOutput, calls=%fused_computation.28.clone.1 | convolution fusion | flops 201359360 | bytes 8536072 | tf_op jit(solution)/shard_map/while/body/eval_jaxpr/fga,fgb->gab/dot_general | solution.py:12
  559.4 12.3 %fusion.63 = f32[8,512]{1,0:T(8,128)S(1)} fusion(f32[8,512,512]{2,1,0:T(8,128)} %fusion.61, f32[8,512]{1,0:T(8,128)S(1)} %fusion.62, f32[512]{0:T(512)S(1)} %get-tuple-element.296, f32[]{:T(128)} %get-tuple-element.295, f32[8,8,512]{2,1,0:T(8,128)S(1)} %gather_fusion.1, pred[8]{0:T(512)(128)(4,1)S(1)} %compare_and_fusion.2, ...), kind=kOutput, calls=%fused_computation.27.clone.1 | convolution fusion | flops 224436224 | bytes 8570893 | tf_op jit(solution)/shard_map/while/body/eval_jaxpr/gab,sgb->sa/dot_general | solution.py:45
  571.9 62.3 %all-reduce = (f32[8]{0:T(128)S(1)}, f32[8]{0:T(128)S(1)}) all-reduce(f32[8]{0:T(128)S(1)} %get-tuple-element.228, f32[8]{0:T(128)S(1)} %get-tuple-element.227), channel_id=1, replica_groups=mesh['row'=16,'col'=8] {'row','col'}, use_global_device_ids=true, to_apply=%region_1.0 | all-reduce | flops 16 | bytes 128 | tf_op jit(solution)/shard_map/psum | solution.py:53
  635.0 63.7 %psum.23 = f32[8]{0:T(128)S(1)} all-reduce(f32[8]{0:T(128)S(1)} %get-tuple-element.222), channel_id=1, replica_groups=mesh['row'=16,'col'=8] {'row','col'}, use_global_device_ids=true, to_apply=%region_9.11 | all-reduce | flops 8 | bytes 64 | tf_op jit(solution)/shard_map/psum | solution.py:58
  (104 shorter events, 51.0 us)
Async XLA Ops:
  7.2 73.5 %all-gather.5.cloned.1.call-start = ((), (), s32[]{:S(2)}) async-start(), calls=%async_computation.1 | async-start | bytes 2113536 | tf_op jit(solution)/shard_map/all_gather | solution.py:29
  8.6 138.0 %all-gather.3.cloned.1.call-start = ((), (), s32[]{:S(2)}) async-start(), calls=%async_computation | async-start | bytes 2113536 | tf_op jit(solution)/shard_map/all_gather | solution.py:30
  146.6 425.1 %copy-start = (f32[8,512]{1,0:T(8,128)S(1)}, f32[8,512]{1,0:T(8,128)}, u32[]{:S(2)}) copy-start(f32[8,512]{1,0:T(8,128)} %param.17) | copy-start | bytes 49156
  146.6 425.1 %copy-start.1 = (f32[8,512]{1,0:T(8,128)S(1)}, f32[8,512]{1,0:T(8,128)}, u32[]{:S(2)}) copy-start(f32[8,512]{1,0:T(8,128)} %param.16) | copy-start | bytes 49156
  146.6 487.6 %copy-start.3 = (f32[8,512]{1,0:T(8,128)S(1)}, f32[8,512]{1,0:T(8,128)}, u32[]{:S(2)}) copy-start(f32[8,512]{1,0:T(8,128)} %param.15) | copy-start | bytes 49156
  635.0 64.4 %copy-start.2 = (f32[8,512]{1,0:T(8,128)}, f32[8,512]{1,0:T(8,128)S(1)}, u32[]{:S(2)}) copy-start(f32[8,512]{1,0:T(8,128)S(1)} %get-tuple-element.223) | copy-start | bytes 49156
Sparse Core Ops, SparseCore 0:
  11.7 68.9 all-gather.4
  83.8 62.7 all-gather.2
where the time goes:
time: 709 us; the launch traced here: 706 us
  matrix products  353 us (50%)
  waiting for transfers between devices  137 us (19%)
  blocking collectives  126 us (18%)
  local copies, waits for them, and re-layouts  68.7 us (10%)
  between operations  14.7 us (2%)
    dot_general x16, matrix products, full_turn(): jnp.einsum('gab,sgb->sa', tiles, dir_right, precision=highest, preferred_...  196 us
    dot_general x16, matrix products, matern_tiles(): jnp.einsum('fga,fgb->gab', left, right, precision=highest, preferred_elem...  157 us
    all_gather x1, waiting for transfers between devices, shards(): lax.all_gather(scaled, ('row', 'col'), axis=1, tiled=True)  70.6 us
    all_gather x1, waiting for transfers between devices, shards(): lax.all_gather(direction, ('row', 'col'), axis=1, tiled=True)  65.9 us
    psum x1, blocking collectives, shards(): lax.psum(jnp.sum(new_residual * new_residual, axis=1), ('row', 'col'))  63.7 us
    psum x1, blocking collectives, shards(): lax.psum((jnp.sum(residual * residual, axis=1), jnp.sum(direction * image...  62.3 us
    gather x16, local copies, waits for them, and re-layouts, full_turn(): tiles = matern_tiles(left, jnp.take(pts_blocks, cols, axis=1), scale_value)  34.4 us
    gather x16, local copies, waits for them, and re-layouts, full_turn(): dir_right = jnp.take(dir_blocks, cols, axis=1)  34.3 us
  transfers between devices with their start and end apart: 2, of which 2 were waited for; matrix products, arithmetic and copies ran while one was open for 0% of the time, Pallas kernels for 0%

commit v1 on v0

v1 whole, which is shorter than its diff:
```python
import jax
import jax.numpy as jnp
from jax import lax
from jax.experimental import pallas as pl
from jax.experimental.pallas import tpu as pltpu
from jax.sharding import PartitionSpec as P

width = 512
per_group = 8
groups = 16
group_pts = width * per_group
depth = 64
chunk = 128
steps = 65
pts_scale = 5.0**0.5 / 3.0
f32, bf16 = jnp.float32, jnp.bfloat16
nt_dims = (((1,), (1,)), ((), ()))
both = ("row", "col")


def dot(left, right):
    return jnp.dot(left, right, preferred_element_type=f32)


def split(value, parts):
    out = []
    for _ in range(parts):
        top = value.astype(bf16).astype(f32)
        out.append(top)
        value = value - top
    return out


def send_kernel(pts_ref, len_ref, dir_ref, out_ref):
    rows = lax.broadcasted_iota(jnp.int32, pts_ref.shape, 0)
    lengths = jnp.zeros(pts_ref.shape, f32)
    for feat in range(8):
        lengths = jnp.where(rows == feat, len_ref[feat], lengths)
    scaled = pts_ref[...] / lengths * pts_scale
    for block in range(per_group):
        out_ref[block, 0:8, :] = scaled
        out_ref[block, 8:16, :] = dir_ref[...]


def norm_rows(pts, first):
    rows = lax.broadcasted_iota(jnp.int32, pts.shape, 0)
    out = jnp.where(rows < 6, 1.0, 0.0)
    for i, part in enumerate(split(jnp.sum(pts * pts, axis=0, keepdims=True), 3)):
        out = jnp.where(rows == first + i, part, out)
    return out


def right_rows(pts):
    one, two, three = split(pts, 3)
    return jnp.concatenate(
        [one, two, one, three, two, one, norm_rows(pts, 3), jnp.zeros_like(pts)], axis=0
    )


def left_rows(pts):
    one, two, three = split(pts * -2.0, 3)
    return jnp.concatenate(
        [one, one, two, one, two, three, norm_rows(pts, 0), jnp.zeros_like(pts)], axis=0
    )


def right_and_dir(block, right_ref, dir_ref, at):
    cols = slice(at * width, (at + 1) * width)
    right_ref[:, cols] = right_rows(block[0:8, :]).astype(bf16)
    dir_ref[:, cols] = jnp.concatenate(split(block[8:16, :], 2), axis=0).astype(bf16)


def own_kernel(own_ref, left_ref, right_ref, dir_ref):
    for at in range(per_group):
        block = own_ref[at]
        left_ref[at * width : (at + 1) * width, :] = left_rows(block[0:8, :]).T.astype(bf16)
        right_and_dir(block, right_ref, dir_ref, at)


def matern(dist):
    dist = jnp.maximum(dist, 1e-30)
    radius = dist * lax.rsqrt(dist)
    decay = jnp.exp2(radius * (-3.0 / 0.6931471805599453))
    return ((dist + 1.0 / 3.0) + radius) * decay


def tile_of(step, group, col):
    pair_row, pair_col = step // 8, 8 + step % 8
    last = step == 64
    diag = jnp.where(col <= 3, 4 + col, 0)
    pair_weight = jnp.where(last, jnp.where(col <= 3, 0.5, 0.0), 1.0)
    pair_row, pair_col = jnp.where(last, diag, pair_row), jnp.where(last, diag, pair_col)
    half_row = step // 4
    half_col = 8 + 2 * (step % 4) + (half_row + group // 8) % 2
    inner = step - 32
    shift = 1 + inner // 8
    on_diag = inner >= 28
    inner_row = jnp.where(on_diag, inner - 28, inner % 8)
    inner_col = jnp.where(on_diag, inner_row, (inner_row + shift) % 8)
    first = step < 32
    own_row = jnp.where(first, half_row, inner_row)
    own_col = jnp.where(first, half_col, inner_col)
    own_weight = jnp.where(on_diag, 0.5, 1.0)
    own = col == 0
    return (
        jnp.where(own, own_row, pair_row),
        jnp.where(own, own_col, pair_col),
        jnp.where(own, own_weight, pair_weight),
    )


def pair_kernel(place_ref, left_ref, own_right_ref, own_dir_ref, other_ref, own_out, other_out,
                right_ref, dir_ref, acc_ref, top_even, low_even, top_odd, low_odd):
    group, col = place_ref[0], place_ref[1]
    right_ref[:, :group_pts] = own_right_ref[...]
    dir_ref[:, :group_pts] = own_dir_ref[...]
    for at in range(per_group):
        right_and_dir(other_ref[at], right_ref, dir_ref, per_group + at)
    acc_ref[...] = jnp.zeros_like(acc_ref)

    def evaluate(step, top, low):
        row, column, _ = tile_of(step, group, col)
        row, column = pl.multiple_of(row * width, width), pl.multiple_of(column * width, width)

        def part(at):
            rows = slice(at * chunk, (at + 1) * chunk)
            tile = matern(
                dot(left_ref[pl.ds(row + at * chunk, chunk), :], right_ref[:, pl.ds(column, width)])
            )
            high = tile.astype(bf16)
            top[rows, :] = high
            low[rows, :] = (tile - high.astype(f32)).astype(bf16)

        return [lambda at=at: part(at) for at in range(width // chunk)]

    def multiply(step, top, low):
        row, column, weight = tile_of(step, group, col)
        row, column = pl.multiple_of(row * width, width), pl.multiple_of(column * width, width)

        def to_column(tile):
            acc_ref[:, pl.ds(column, width)] += weight * dot(
                dir_ref[:, pl.ds(row, width)], tile[...]
            )

        def to_row(tile):
            acc_ref[:, pl.ds(row, width)] += weight * lax.dot_general(
                dir_ref[:, pl.ds(column, width)], tile[...], nt_dims, preferred_element_type=f32
            )

        return [
            lambda: to_column(top), lambda: to_column(low), lambda: to_row(top), lambda: to_row(low)
        ]

    def run(first, second):
        for one, two in zip(first, second, strict=True):
            one()
            two()

    for part in evaluate(0, top_even, low_even):
        part()

    def turn(index, carry):
        step = 2 * index
        run(evaluate(step + 1, top_odd, low_odd), multiply(step, top_even, low_even))
        run(evaluate(step + 2, top_even, low_even), multiply(step + 1, top_odd, low_odd))
        return carry

    lax.fori_loop(0, steps // 2, turn, 0)
    for part in multiply(steps - 1, top_even, low_even):
        part()
    for at in range(per_group):
        cols = slice(at * width, (at + 1) * width)
        own_out[at] = acc_ref[0:8, cols] + acc_ref[8:16, cols]
        cols = slice(group_pts + at * width, group_pts + (at + 1) * width)
        other_out[at] = acc_ref[0:8, cols] + acc_ref[8:16, cols]


def image_kernel(scale_ref, noise_ref, parts_ref, dir_ref, res_ref, image_ref, sums_ref):
    product = parts_ref[0]
    for at in range(1, per_group):
        product = product + parts_ref[at]
    direction, residual = dir_ref[...], res_ref[...]
    image = (3.0 * scale_ref[0]) * product + noise_ref[0] * direction
    image_ref[...] = image
    rows = lax.broadcasted_iota(jnp.int32, (8, 128), 0)
    lanes = lax.broadcasted_iota(jnp.int32, (8, 128), 1)
    packed = jnp.zeros((8, 128), f32)
    pairs = ((residual, residual), (direction, image), (residual, image), (image, image))
    for i, (one, two) in enumerate(pairs):
        packed = jnp.where(lanes == 8 * i + rows, jnp.sum(one * two, axis=1, keepdims=True), packed)
    sums_ref[...] = jnp.broadcast_to(jnp.sum(packed, axis=0, keepdims=True), sums_ref.shape)


def update_kernel(sums_ref, image_ref, sol_ref, res_ref, dir_ref, new_sol, new_res, new_dir):
    total = jnp.sum(sums_ref[...], axis=0, keepdims=True)
    rows = lax.broadcasted_iota(jnp.int32, (8, 128), 0)
    lanes = lax.broadcasted_iota(jnp.int32, (8, 128), 1)
    rr_old, curv, res_image, image_sq = (
        jnp.sum(jnp.where(lanes == 8 * i + rows, total, 0.0), axis=1, keepdims=True)
        for i in range(4)
    )
    alpha = rr_old / curv
    rr_new = rr_old - alpha * (2.0 * res_image - alpha * image_sq)
    direction = dir_ref[...]
    residual = res_ref[...] - alpha * image_ref[...]
    new_sol[...] = sol_ref[...] + alpha * direction
    new_res[...] = residual
    new_dir[...] = residual + (rr_new / rr_old) * direction


def call(kernel, outs, *args, smem=0, scratch=(), limit=16 << 20, cost=None):
    vmem, scalars = pl.BlockSpec(memory_space=pltpu.VMEM), pl.BlockSpec(memory_space=pltpu.SMEM)
    many = isinstance(outs, list)
    return pl.pallas_call(
        kernel,
        out_shape=outs,
        in_specs=[scalars if i < smem else vmem for i in range(len(args))],
        out_specs=[vmem] * len(outs) if many else vmem,
        scratch_shapes=scratch,
        cost_estimate=cost,
        compiler_params=pltpu.CompilerParams(vmem_limit_bytes=limit),
    )(*args)


def shards(points, lengthscale, outputscale, noise, solution, residual, direction):
    def array(*shape, dtype=f32):
        return jax.ShapeDtypeStruct(shape, dtype)

    def partner(group, col):
        return (group + (col if col else groups // 2)) % groups

    def send_body(len_ref, pts_ref, dir_ref, out_ref):
        send_kernel(pts_ref, len_ref, dir_ref, out_ref)

    sent = call(
        send_body, array(per_group, 16, width), lengthscale, points, direction, smem=1
    )
    own = lax.all_to_all(sent, "col", split_axis=0, concat_axis=0)
    places = [(group, col) for group in range(groups) for col in range(per_group)]
    fetch = [
        (partner(group, col) * per_group + col, group * per_group + col) for group, col in places
    ]
    other = lax.ppermute(own, both, fetch)
    left, own_right, own_dir = call(
        own_kernel,
        [
            array(group_pts, depth, dtype=bf16),
            array(depth, group_pts, dtype=bf16),
            array(16, group_pts, dtype=bf16),
        ],
        own,
    )
    place = jnp.stack([lax.axis_index("row"), lax.axis_index("col")]).astype(jnp.int32)
    tile = pltpu.VMEM((width, width), bf16)
    own_out, other_out = call(
        pair_kernel,
        [array(per_group, 8, width), array(per_group, 8, width)],
        place, left, own_right, own_dir, other,
        smem=1,
        scratch=[
            pltpu.VMEM((depth, 2 * group_pts), bf16),
            pltpu.VMEM((16, 2 * group_pts), bf16),
            pltpu.VMEM((16, 2 * group_pts), f32),
            tile, tile, tile, tile,
        ],
        limit=32 << 20,
    )
    back = lax.ppermute(other_out, both, [(to, source) for source, to in fetch])
    parts = lax.all_to_all(own_out + back, "col", split_axis=0, concat_axis=0)
    image, sums = call(
        image_kernel,
        [array(8, width), array(groups * per_group, 128)],
        outputscale, noise, parts, direction, residual,
        smem=2,
    )
    sums = lax.all_to_all(sums, both, split_axis=0, concat_axis=0, tiled=True)
    return tuple(
        call(
            update_kernel,
            [array(8, width)] * 3,
            sums, image, solution, residual, direction,
        )
    )


def solution(mesh):
    spread = P(None, both)
    return jax.shard_map(
        shards,
        mesh=mesh,
        in_specs=(spread, P(), P(), P(), spread, spread, spread),
        out_specs=(spread, spread, spread),
        check_vma=False,
    )
```

time: 709 us -> 107 us (0.15)
  matrix products: 353 us -> 0 us
  waiting for transfers between devices: 137 us -> 16.3 us
  blocking collectives: 126 us -> 29.7 us
  local copies, waits for them, and re-layouts: 68.7 us -> 2.1 us
  Pallas kernels: 0 us -> 44.8 us
  between operations: 14.7 us -> 1.99 us
  starting transfers between devices: 0.08 us -> 10.4 us
    dot_general x32 -> x0, matrix products: 353 us -> none  [the longest x16 196 us: full_turn(): jnp.einsum('gab,sgb->sa', tiles, dir_right, precision=highest, preferred_...]
    all_gather x2 -> x0, waiting for transfers between devices: 137 us -> none  [the longest x1 70.6 us: shards(): lax.all_gather(scaled, ('row', 'col'), axis=1, tiled=True)]
    psum x2 -> x0, blocking collectives: 126 us -> none  [the longest x1 63.7 us: shards(): lax.psum(jnp.sum(new_residual * new_residual, axis=1), ('row', 'col'))]
    gather x32 -> x0, local copies, waits for them, and re-layouts: 68.7 us -> none  [the longest x16 34.4 us: full_turn(): tiles = matern_tiles(left, jnp.take(pts_blocks, cols, axis=1), scale_value)]
    pallas_call x0 -> x5, Pallas kernels: none -> 44.8 us  [call(): pl.pallas_call(kernel, out_shape=outs, in_specs=[scalars if i < smem else...]
    all_to_all x0 -> x2, blocking collectives: none -> 29.7 us  [the longest x1 17.4 us: shards(): sums = lax.all_to_all(sums, both, split_axis=0, concat_axis=0, tiled=True)]
    ppermute x0 -> x2, waiting for transfers between devices: none -> 12.4 us  [the longest x1 9.19 us: shards(): back = lax.ppermute(other_out, both, [(to, source) for source, to in fetch])]
  transfers between devices with their start and end apart: 2 -> 3, of which waited for: 2 -> 3; matrix products, arithmetic and copies ran while one was open for 0% -> 0% of each run, Pallas kernels for 0% -> 0%
where the time goes in v1:
time: 107 us; the launch traced here: 106 us
  Pallas kernels  44.8 us (42%)
  blocking collectives  29.7 us (28%)
  waiting for transfers between devices  16.3 us (15%)
  starting transfers between devices  10.4 us (10%)
  local copies, waits for them, and re-layouts  2.1 us (2%)
  between operations  1.99 us (2%)
    pallas_call x5, Pallas kernels, call(): pl.pallas_call(kernel, out_shape=outs, in_specs=[scalars if i < smem else...  44.8 us
    all_to_all x1, blocking collectives, shards(): sums = lax.all_to_all(sums, both, split_axis=0, concat_axis=0, tiled=True)  17.4 us
    all_to_all x1, blocking collectives, shards(): own = lax.all_to_all(sent, 'col', split_axis=0, concat_axis=0)  12.3 us
    ppermute x1, waiting for transfers between devices, shards(): back = lax.ppermute(other_out, both, [(to, source) for source, to in fetch])  9.19 us
    ppermute x1, starting transfers between devices, shards(): other = lax.ppermute(own, both, fetch)  5.95 us
    all_to_all x1, starting transfers between devices, shards(): parts = lax.all_to_all(own_out + back, 'col', split_axis=0, concat_axis=0)  4.38 us
    all_to_all x1, waiting for transfers between devices, shards(): parts = lax.all_to_all(own_out + back, 'col', split_axis=0, concat_axis=0)  3.98 us
    ppermute x1, waiting for transfers between devices, shards(): other = lax.ppermute(own, both, fetch)  3.17 us
  transfers between devices with their start and end apart: 3, of which 3 were waited for; matrix products, arithmetic and copies ran while one was open for 0% of the time, Pallas kernels for 0%

profile of v1, /device:TPU:1, one launch (start us, length us, event | category | flops | bytes accessed | tf_op | source)
XLA Modules:
  0.0 106.1 jit_solution(6892518786503600381)
XLA Ops:
  0.6 0.0 copy-start
  0.6 0.7 copy-done
  1.4 0.0 copy-start.3
  1.4 0.7 copy-done.3
  2.1 0.0 copy-start.5
  2.1 0.7 copy-done.5
  2.7 0.6 shard_map.94
  3.3 12.3 %all_to_all.21.own_ref = f32[8,16,512]{2,1,0:T(8,128)S(1)} all-to-all(f32[8,16,512]{2,1,0:T(8,128)S(1)} %shard_map.94), channel_id=1, replica_groups=mesh['row'=16,'col'=8] {'col'}, dimensions={0} | all-to-all | bytes 524288 | tf_op jit(solution)/shard_map/all_to_all | solution.py:238
  15.6 6.0 %collective-permute-start = (f32[8,16,512]{2,1,0:T(8,128)S(1)}, f32[8,16,512]{2,1,0:T(8,128)S(1)}, u32[]{:S(2)}, u32[]{:S(2)}) collective-permute-start(f32[8,16,512]{2,1,0:T(8,128)S(1)} %all_to_all.21.own_ref), channel_id=1, source_target_pairs={{64,0},{9,1},{18,2},{27,3},{36,4},{45,5},{54,6},{63,7},{72,8},{17,... | collective-permute-start | bytes 786440 | tf_op jit(solution)/shard_map/ppermute | solution.py:243
  21.5 0.1 pad_add_fusion.place_ref
  21.6 0.4 shard_map.95
  22.0 3.2 %collective-permute-done.other_ref = f32[8,16,512]{2,1,0:T(8,128)S(1)} collective-permute-done((f32[8,16,512]{2,1,0:T(8,128)S(1)}, f32[8,16,512]{2,1,0:T(8,128)S(1)}, u32[]{:S(2)}, u32[]{:S(2)}) %collective-permute-start) | collective-permute-done | bytes 262176 | tf_op jit(solution)/shard_map/ppermute | solution.py:243
  25.2 43.0 %shard_map.96 = (f32[8,8,512]{2,1,0:T(8,128)S(1)}, f32[8,8,512]{2,1,0:T(8,128)S(1)}) custom-call(s32[2]{0:T(128)S(1)} %pad_add_fusion.place_ref, bf16[4096,64]{1,0:T(8,128)(2,1)S(1)} %get-tuple-element.10.left_ref, bf16[64,4096]{1,0:T(8,128)(2,1)S(1)} %get-tuple-element.11.own_right_ref, bf16[16,4096]{1,0:T(8,128)(2,1)S(1)} %get-tuple-element.12.own_dir_ref, ...), custom_call_target="tpu_custom_call" | custom-call | tf_op jit(solution)/shard_map/pallas_call | solution.py:214
  68.2 0.1 collective-permute-start.1
  68.3 9.2 %collective-permute-done.1 = f32[8,8,512]{2,1,0:T(8,128)S(1)} collective-permute-done((f32[8,8,512]{2,1,0:T(8,128)S(1)}, f32[8,8,512]{2,1,0:T(8,128)S(1)}, u32[]{:S(2)}, u32[]{:S(2)}) %collective-permute-start.1) | collective-permute-done | bytes 131104 | tf_op jit(solution)/shard_map/ppermute | solution.py:268
  77.5 0.7 add.3
  78.2 0.0 copy-start.1
  78.2 0.0 copy-start.2
  78.2 4.4 %all-to-all-start.1 = ((f32[8,8,512]{2,1,0:T(8,128)}), f32[8,8,512]{2,1,0:T(8,128)S(1)}, u32[]{:S(2)}, u32[]{:S(2)}) async-start(f32[8,8,512]{2,1,0:T(8,128)} %add.3), calls=%async_computation.1 | async-start | bytes 262144 | tf_op jit(solution)/shard_map/all_to_all | solution.py:269
  83.8 4.0 %all-to-all-done.1.parts_ref = f32[8,8,512]{2,1,0:T(8,128)S(1)} async-done(((f32[8,8,512]{2,1,0:T(8,128)}), f32[8,8,512]{2,1,0:T(8,128)S(1)}, u32[]{:S(2)}, u32[]{:S(2)}) %all-to-all-start.1) | async-done | bytes 131104 | tf_op jit(solution)/shard_map/all_to_all | solution.py:269
  87.8 0.0 copy-done.1
  87.8 0.0 copy-done.2
  87.8 0.1 shard_map.97
  87.9 0.0 copy-start.4
  87.9 17.4 %all_to_all.22 = f32[128,1,128]{2,1,0:T(1,128)S(1)} all-to-all(f32[128,1,128]{2,1,0:T(1,128)S(1)} %bitcast.7), channel_id=1, replica_groups=mesh['row'=16,'col'=8] {'row','col'}, dimensions={0} | all-to-all | bytes 131072 | tf_op jit(solution)/shard_map/all_to_all | solution.py:276
  105.4 0.0 copy-done.4
  105.4 0.7 shard_map.98
Async XLA Ops:
  0.6 0.7 copy-start
  1.4 0.7 copy-start.3
  2.1 0.7 copy-start.5
  15.6 9.6 %collective-permute-start = (f32[8,16,512]{2,1,0:T(8,128)S(1)}, f32[8,16,512]{2,1,0:T(8,128)S(1)}, u32[]{:S(2)}, u32[]{:S(2)}) collective-permute-start(f32[8,16,512]{2,1,0:T(8,128)S(1)} %all_to_all.21.own_ref), channel_id=1, source_target_pairs={{64,0},{9,1},{18,2},{27,3},{36,4},{45,5},{54,6},{63,7},{72,8},{17,... | collective-permute-start | bytes 786440 | tf_op jit(solution)/shard_map/ppermute | solution.py:243
  68.2 9.3 %collective-permute-start.1 = (f32[8,8,512]{2,1,0:T(8,128)S(1)}, f32[8,8,512]{2,1,0:T(8,128)S(1)}, u32[]{:S(2)}, u32[]{:S(2)}) collective-permute-start(f32[8,8,512]{2,1,0:T(8,128)S(1)} %get-tuple-element.14), channel_id=1, source_target_pairs={{0,64},{1,9},{2,18},{3,27},{4,36},{5,45},{6,54},{7,63},{8,72},{9,1... | collective-permute-start | bytes 393224 | tf_op jit(solution)/shard_map/ppermute | solution.py:268
  78.2 9.7 %copy-start.1 = (f32[8,512]{1,0:T(8,128)S(1)}, f32[8,512]{1,0:T(8,128)}, u32[]{:S(2)}) copy-start(f32[8,512]{1,0:T(8,128)} %dir_ref.5) | copy-start | bytes 49156
  78.2 9.7 %copy-start.2 = (f32[8,512]{1,0:T(8,128)S(1)}, f32[8,512]{1,0:T(8,128)}, u32[]{:S(2)}) copy-start(f32[8,512]{1,0:T(8,128)} %res_ref.3) | copy-start | bytes 49156
  78.2 9.7 %all-to-all-start.1 = ((f32[8,8,512]{2,1,0:T(8,128)}), f32[8,8,512]{2,1,0:T(8,128)S(1)}, u32[]{:S(2)}, u32[]{:S(2)}) async-start(f32[8,8,512]{2,1,0:T(8,128)} %add.3), calls=%async_computation.1 | async-start | bytes 262144 | tf_op jit(solution)/shard_map/all_to_all | solution.py:269
  87.9 17.5 %copy-start.4 = (f32[8,512]{1,0:T(8,128)S(1)}, f32[8,512]{1,0:T(8,128)}, u32[]{:S(2)}) copy-start(f32[8,512]{1,0:T(8,128)} %sol_ref.1) | copy-start | bytes 49156

commit v2 on v1

--- a/solution.py
+++ b/solution.py
@@ -31,15 +31,30 @@
     return out
 
 
-def send_kernel(pts_ref, len_ref, dir_ref, out_ref):
-    rows = lax.broadcasted_iota(jnp.int32, pts_ref.shape, 0)
-    lengths = jnp.zeros(pts_ref.shape, f32)
+def send_kernel(pts_hbm, len_hbm, dir_hbm, out_ref, pts_ref, len_ref, dir_ref, sems):
+    pairs = ((pts_hbm, pts_ref), (len_hbm, len_ref), (dir_hbm, dir_ref))
+    copies = [pltpu.make_async_copy(*pair, sems.at[i]) for i, pair in enumerate(pairs)]
+    for copy in copies:
+        copy.start()
+    for copy in copies:
+        copy.wait()
+    scaled = pts_ref[...] / lengths_of(len_ref) * pts_scale
+    direction = dir_ref[...]
+    for block in range(per_group):
+        out_ref[block, 0:8, :] = scaled
+        out_ref[block, 8:16, :] = direction
+
+
+def lengths_of(len_ref):
+    rows = lax.broadcasted_iota(jnp.int32, (8, width), 0)
+    lengths = jnp.zeros((8, width), f32)
     for feat in range(8):
         lengths = jnp.where(rows == feat, len_ref[feat], lengths)
-    scaled = pts_ref[...] / lengths * pts_scale
-    for block in range(per_group):
-        out_ref[block, 0:8, :] = scaled
-        out_ref[block, 8:16, :] = dir_ref[...]
+    return lengths
+
+
+def add_kernel(one_ref, two_ref, out_ref):
+    out_ref[...] = one_ref[...] + two_ref[...]
 
 
 def norm_rows(pts, first):
@@ -64,17 +79,17 @@
     )
 
 
-def right_and_dir(block, right_ref, dir_ref, at):
+def right_and_dir(pts, direction, right_ref, dir_ref, at):
     cols = slice(at * width, (at + 1) * width)
-    right_ref[:, cols] = right_rows(block[0:8, :]).astype(bf16)
-    dir_ref[:, cols] = jnp.concatenate(split(block[8:16, :], 2), axis=0).astype(bf16)
+    right_ref[:, cols] = right_rows(pts).astype(bf16)
+    dir_ref[:, cols] = jnp.concatenate(split(direction, 2), axis=0).astype(bf16)
 
 
 def own_kernel(own_ref, left_ref, right_ref, dir_ref):
     for at in range(per_group):
-        block = own_ref[at]
-        left_ref[at * width : (at + 1) * width, :] = left_rows(block[0:8, :]).T.astype(bf16)
-        right_and_dir(block, right_ref, dir_ref, at)
+        pts = own_ref[at, 0:8, :]
+        left_ref[at * width : (at + 1) * width, :] = left_rows(pts).T.astype(bf16)
+        right_and_dir(pts, own_ref[at, 8:16, :], right_ref, dir_ref, at)
 
 
 def matern(dist):
@@ -115,7 +130,7 @@
     right_ref[:, :group_pts] = own_right_ref[...]
     dir_ref[:, :group_pts] = own_dir_ref[...]
     for at in range(per_group):
-        right_and_dir(other_ref[at], right_ref, dir_ref, per_group + at)
+        right_and_dir(other_ref[at, 0:8, :], other_ref[at, 8:16, :], right_ref, dir_ref, per_group + at)
     acc_ref[...] = jnp.zeros_like(acc_ref)
 
     def evaluate(step, top, low):
@@ -148,7 +163,7 @@
             )
 
         return [
-            lambda: to_column(top), lambda: to_column(low), lambda: to_row(top), lambda: to_row(low)
+            lambda: to_row(top), lambda: to_column(top), lambda: to_row(low), lambda: to_column(low)
         ]
 
     def run(first, second):
@@ -165,7 +180,7 @@
         run(evaluate(step + 2, top_even, low_even), multiply(step + 1, top_odd, low_odd))
         return carry
 
-    lax.fori_loop(0, steps // 2, turn, 0)
+    lax.fori_loop(0, steps // 2, turn, 0, unroll=4)
     for part in multiply(steps - 1, top_even, low_even):
         part()
     for at in range(per_group):
@@ -229,12 +244,19 @@
     def partner(group, col):
         return (group + (col if col else groups // 2)) % groups
 
-    def send_body(len_ref, pts_ref, dir_ref, out_ref):
-        send_kernel(pts_ref, len_ref, dir_ref, out_ref)
-
-    sent = call(
-        send_body, array(per_group, 16, width), lengthscale, points, direction, smem=1
-    )
+    sent = pl.pallas_call(
+        send_kernel,
+        out_shape=array(per_group, 16, width),
+        in_specs=[pl.BlockSpec(memory_space=pltpu.HBM)] * 3,
+        out_specs=pl.BlockSpec(memory_space=pltpu.VMEM),
+        scratch_shapes=[
+            pltpu.VMEM((8, width), f32),
+            pltpu.SMEM((8,), f32),
+            pltpu.VMEM((8, width), f32),
+            pltpu.SemaphoreType.DMA((3,)),
+        ],
+        compiler_params=pltpu.CompilerParams(vmem_limit_bytes=62 << 20),
+    )(points, lengthscale, direction)
     own = lax.all_to_all(sent, "col", split_axis=0, concat_axis=0)
     places = [(group, col) for group in range(groups) for col in range(per_group)]
     fetch = [
@@ -266,7 +288,8 @@
         limit=32 << 20,
     )
     back = lax.ppermute(other_out, both, [(to, source) for source, to in fetch])
-    parts = lax.all_to_all(own_out + back, "col", split_axis=0, concat_axis=0)
+    total = call(add_kernel, array(per_group, 8, width), own_out, back)
+    parts = lax.all_to_all(total, "col", split_axis=0, concat_axis=0)
     image, sums = call(
         image_kernel,
         [array(8, width), array(groups * per_group, 128)],

time: 107 us -> 101 us (0.944)
  Pallas kernels: 44.8 us -> 42 us
  local copies, waits for them, and re-layouts: 2.1 us -> 0.01 us
    pallas_call x5, Pallas kernels: 44.8 us -> 40.4 us  [call(): pl.pallas_call(kernel, out_shape=outs, in_specs=[scalars if i < smem else...]
    unnamed x12 -> x6, local copies, waits for them, and re-layouts: 2.1 us -> 0.01 us
    pallas_call x0 -> x1, Pallas kernels: none -> 1.54 us  [shards(): pl.pallas_call(send_kernel, out_shape=array(per_group, 16, width), in_spe...]
where the time goes in v2:
time: 101 us
  Pallas kernels  42 us (42%)
  blocking collectives  29.9 us (30%)
  waiting for transfers between devices  16.3 us (16%)
  starting transfers between devices  10.4 us (10%)
  between operations  1.98 us (2%)
    pallas_call x5, Pallas kernels, call(): pl.pallas_call(kernel, out_shape=outs, in_specs=[scalars if i < smem else...  40.4 us
    all_to_all x1, blocking collectives, shards(): sums = lax.all_to_all(sums, both, split_axis=0, concat_axis=0, tiled=True)  17.4 us
    all_to_all x1, blocking collectives, shards(): own = lax.all_to_all(sent, 'col', split_axis=0, concat_axis=0)  12.5 us
    ppermute x1, waiting for transfers between devices, shards(): back = lax.ppermute(other_out, both, [(to, source) for source, to in fetch])  9.19 us
    ppermute x1, starting transfers between devices, shards(): other = lax.ppermute(own, both, fetch)  5.95 us
    all_to_all x1, starting transfers between devices, shards(): parts = lax.all_to_all(total, 'col', split_axis=0, concat_axis=0)  4.38 us
    all_to_all x1, waiting for transfers between devices, shards(): parts = lax.all_to_all(total, 'col', split_axis=0, concat_axis=0)  3.98 us
    ppermute x1, waiting for transfers between devices, shards(): other = lax.ppermute(own, both, fetch)  3.17 us
  transfers between devices with their start and end apart: 3, of which 3 were waited for; matrix products, arithmetic and copies ran while one was open for 0% of the time, Pallas kernels for 0%

profile of v2, /device:TPU:1, one launch (start us, length us, event | category | flops | bytes accessed | tf_op | source)
XLA Modules:
  0.0 100.7 jit_solution(1851402111093220782)
XLA Ops:
  0.6 1.5 %shard_map.94 = f32[8,16,512]{2,1,0:T(8,128)} custom-call(f32[8,512]{1,0:T(8,128)} %pts_hbm.1, f32[8]{0:T(128)} %len_hbm.1, f32[8,512]{1,0:T(8,128)} %dir_ref.3), custom_call_target="tpu_custom_call" | custom-call | tf_op jit(solution)/shard_map/pallas_call | solution.py:247
  2.2 12.5 %all_to_all.21.own_ref = f32[8,16,512]{2,1,0:T(8,128)S(1)} all-to-all(f32[8,16,512]{2,1,0:T(8,128)} %shard_map.94), channel_id=1, replica_groups=mesh['row'=16,'col'=8] {'col'}, dimensions={0} | all-to-all | bytes 524288 | tf_op jit(solution)/shard_map/all_to_all | solution.py:260
  14.7 6.0 %collective-permute-start = (f32[8,16,512]{2,1,0:T(8,128)S(1)}, f32[8,16,512]{2,1,0:T(8,128)S(1)}, u32[]{:S(2)}, u32[]{:S(2)}) collective-permute-start(f32[8,16,512]{2,1,0:T(8,128)S(1)} %all_to_all.21.own_ref), channel_id=1, source_target_pairs={{64,0},{9,1},{18,2},{27,3},{36,4},{45,5},{54,6},{63,7},{72,8},{17,... | collective-permute-start | bytes 786440 | tf_op jit(solution)/shard_map/ppermute | solution.py:265
  20.6 0.1 pad_add_fusion.place_ref
  20.7 0.4 shard_map.95
  21.1 3.2 %collective-permute-done.other_ref = f32[8,16,512]{2,1,0:T(8,128)S(1)} collective-permute-done((f32[8,16,512]{2,1,0:T(8,128)S(1)}, f32[8,16,512]{2,1,0:T(8,128)S(1)}, u32[]{:S(2)}, u32[]{:S(2)}) %collective-permute-start) | collective-permute-done | bytes 262176 | tf_op jit(solution)/shard_map/ppermute | solution.py:265
  24.3 38.6 %shard_map.96 = (f32[8,8,512]{2,1,0:T(8,128)S(1)}, f32[8,8,512]{2,1,0:T(8,128)S(1)}) custom-call(s32[2]{0:T(128)S(1)} %pad_add_fusion.place_ref, bf16[4096,64]{1,0:T(8,128)(2,1)S(1)} %get-tuple-element.10.left_ref, bf16[64,4096]{1,0:T(8,128)(2,1)S(1)} %get-tuple-element.11.own_right_ref, bf16[16,4096]{1,0:T(8,128)(2,1)S(1)} %get-tuple-element.12.own_dir_ref, ...), custom_call_target="tpu_custom_call" | custom-call | tf_op jit(solution)/shard_map/pallas_call | solution.py:229
  62.8 0.1 collective-permute-start.1
  62.9 9.2 %collective-permute-done.1.two_ref = f32[8,8,512]{2,1,0:T(8,128)S(1)} collective-permute-done((f32[8,8,512]{2,1,0:T(8,128)S(1)}, f32[8,8,512]{2,1,0:T(8,128)S(1)}, u32[]{:S(2)}, u32[]{:S(2)}) %collective-permute-start.1) | collective-permute-done | bytes 131104 | tf_op jit(solution)/shard_map/ppermute | solution.py:290
  72.1 0.7 shard_map.97
  72.8 0.0 copy-start
  72.8 0.0 copy-start.1
  72.8 4.4 %all-to-all-start.1 = ((f32[8,8,512]{2,1,0:T(8,128)}), f32[8,8,512]{2,1,0:T(8,128)S(1)}, u32[]{:S(2)}, u32[]{:S(2)}) async-start(f32[8,8,512]{2,1,0:T(8,128)} %shard_map.97), calls=%async_computation.1 | async-start | bytes 262144 | tf_op jit(solution)/shard_map/all_to_all | solution.py:292
  78.5 4.0 %all-to-all-done.1.parts_ref = f32[8,8,512]{2,1,0:T(8,128)S(1)} async-done(((f32[8,8,512]{2,1,0:T(8,128)}), f32[8,8,512]{2,1,0:T(8,128)S(1)}, u32[]{:S(2)}, u32[]{:S(2)}) %all-to-all-start.1) | async-done | bytes 131104 | tf_op jit(solution)/shard_map/all_to_all | solution.py:292
  82.4 0.0 copy-done
  82.4 0.0 copy-done.1
  82.4 0.1 shard_map.98
  82.5 0.0 copy-start.2
  82.6 17.4 %all_to_all.22 = f32[128,1,128]{2,1,0:T(1,128)S(1)} all-to-all(f32[128,1,128]{2,1,0:T(1,128)S(1)} %bitcast.7), channel_id=1, replica_groups=mesh['row'=16,'col'=8] {'row','col'}, dimensions={0} | all-to-all | bytes 131072 | tf_op jit(solution)/shard_map/all_to_all | solution.py:299
  100.0 0.0 copy-done.2
  100.0 0.7 shard_map.99
Async XLA Ops:
  14.7 9.6 %collective-permute-start = (f32[8,16,512]{2,1,0:T(8,128)S(1)}, f32[8,16,512]{2,1,0:T(8,128)S(1)}, u32[]{:S(2)}, u32[]{:S(2)}) collective-permute-start(f32[8,16,512]{2,1,0:T(8,128)S(1)} %all_to_all.21.own_ref), channel_id=1, source_target_pairs={{64,0},{9,1},{18,2},{27,3},{36,4},{45,5},{54,6},{63,7},{72,8},{17,... | collective-permute-start | bytes 786440 | tf_op jit(solution)/shard_map/ppermute | solution.py:265
  62.8 9.3 %collective-permute-start.1 = (f32[8,8,512]{2,1,0:T(8,128)S(1)}, f32[8,8,512]{2,1,0:T(8,128)S(1)}, u32[]{:S(2)}, u32[]{:S(2)}) collective-permute-start(f32[8,8,512]{2,1,0:T(8,128)S(1)} %get-tuple-element.14), channel_id=1, source_target_pairs={{0,64},{1,9},{2,18},{3,27},{4,36},{5,45},{6,54},{7,63},{8,72},{9,1... | collective-permute-start | bytes 393224 | tf_op jit(solution)/shard_map/ppermute | solution.py:290
  72.8 9.7 %copy-start = (f32[8,512]{1,0:T(8,128)S(1)}, f32[8,512]{1,0:T(8,128)}, u32[]{:S(2)}) copy-start(f32[8,512]{1,0:T(8,128)} %dir_ref.3) | copy-start | bytes 49156
  72.8 9.7 %copy-start.1 = (f32[8,512]{1,0:T(8,128)S(1)}, f32[8,512]{1,0:T(8,128)}, u32[]{:S(2)}) copy-start(f32[8,512]{1,0:T(8,128)} %res_ref.3) | copy-start | bytes 49156
  72.8 9.7 %all-to-all-start.1 = ((f32[8,8,512]{2,1,0:T(8,128)}), f32[8,8,512]{2,1,0:T(8,128)S(1)}, u32[]{:S(2)}, u32[]{:S(2)}) async-start(f32[8,8,512]{2,1,0:T(8,128)} %shard_map.97), calls=%async_computation.1 | async-start | bytes 262144 | tf_op jit(solution)/shard_map/all_to_all | solution.py:292
  82.5 17.5 %copy-start.2 = (f32[8,512]{1,0:T(8,128)S(1)}, f32[8,512]{1,0:T(8,128)}, u32[]{:S(2)}) copy-start(f32[8,512]{1,0:T(8,128)} %sol_ref.1) | copy-start | bytes 49156

commit v3 on v2

--- a/solution.py
+++ b/solution.py
@@ -11,7 +11,7 @@
 group_pts = width * per_group
 depth = 64
 chunk = 128
-steps = 65
+half_col = 4
 pts_scale = 5.0**0.5 / 3.0
 f32, bf16 = jnp.float32, jnp.bfloat16
 nt_dims = (((1,), (1,)), ((), ()))
@@ -85,7 +85,9 @@
     dir_ref[:, cols] = jnp.concatenate(split(direction, 2), axis=0).astype(bf16)
 
 
-def own_kernel(own_ref, left_ref, right_ref, dir_ref):
+def own_kernel(scale_ref, noise_ref, own_ref, left_ref, right_ref, dir_ref, factor_ref):
+    rows = lax.broadcasted_iota(jnp.int32, factor_ref.shape, 0)
+    factor_ref[...] = jnp.where(rows == 0, 3.0 * scale_ref[0], noise_ref[0])
     for at in range(per_group):
         pts = own_ref[at, 0:8, :]
         left_ref[at * width : (at + 1) * width, :] = left_rows(pts).T.astype(bf16)
@@ -100,27 +102,19 @@
 
 
 def tile_of(step, group, col):
-    pair_row, pair_col = step // 8, 8 + step % 8
-    last = step == 64
-    diag = jnp.where(col <= 3, 4 + col, 0)
-    pair_weight = jnp.where(last, jnp.where(col <= 3, 0.5, 0.0), 1.0)
-    pair_row, pair_col = jnp.where(last, diag, pair_row), jnp.where(last, diag, pair_col)
-    half_row = step // 4
-    half_col = 8 + 2 * (step % 4) + (half_row + group // 8) % 2
-    inner = step - 32
-    shift = 1 + inner // 8
-    on_diag = inner >= 28
-    inner_row = jnp.where(on_diag, inner - 28, inner % 8)
-    inner_col = jnp.where(on_diag, inner_row, (inner_row + shift) % 8)
-    first = step < 32
-    own_row = jnp.where(first, half_row, inner_row)
-    own_col = jnp.where(first, half_col, inner_col)
-    own_weight = jnp.where(on_diag, 0.5, 1.0)
-    own = col == 0
+    halved = col == half_col
+    pairs = jnp.where(halved, 32, 64)
+    pair_row = jnp.where(halved, step // 4, step // 8)
+    pair_col = 8 + jnp.where(halved, 2 * (step % 4) + (pair_row + group // 8) % 2, step % 8)
+    inner = step - pairs + jnp.where(halved, 7, jnp.where(col > half_col, col - 1, col))
+    alone = inner >= 28
+    row = jnp.where(alone, inner - 28, inner % 8)
+    column = jnp.where(alone, row, (row + 1 + inner // 8) % 8)
+    mixed = step < pairs
     return (
-        jnp.where(own, own_row, pair_row),
-        jnp.where(own, own_col, pair_col),
-        jnp.where(own, own_weight, pair_weight),
+        jnp.where(mixed, pair_row, row),
+        jnp.where(mixed, pair_col, column),
+        jnp.where(jnp.logical_and(alone, jnp.logical_not(mixed)), 0.5, 1.0),
     )
 
 
@@ -180,8 +174,14 @@
         run(evaluate(step + 2, top_even, low_even), multiply(step + 1, top_odd, low_odd))
         return carry
 
-    lax.fori_loop(0, steps // 2, turn, 0, unroll=4)
-    for part in multiply(steps - 1, top_even, low_even):
+    lax.fori_loop(0, 28, turn, 0, unroll=4)
+    halved = col == half_col
+
+    def last_turns(index, carry):
+        return turn(2 * index + 29, turn(2 * index + 28, carry))
+
+    lax.fori_loop(0, jnp.where(halved, 1, 2), last_turns, 0)
+    for part in multiply(jnp.where(halved, 60, 64), top_even, low_even):
         part()
     for at in range(per_group):
         cols = slice(at * width, (at + 1) * width)
@@ -190,12 +190,12 @@
         other_out[at] = acc_ref[0:8, cols] + acc_ref[8:16, cols]
 
 
-def image_kernel(scale_ref, noise_ref, parts_ref, dir_ref, res_ref, image_ref, sums_ref):
+def image_kernel(factor_ref, parts_ref, dir_ref, res_ref, image_ref, sums_ref):
     product = parts_ref[0]
     for at in range(1, per_group):
         product = product + parts_ref[at]
     direction, residual = dir_ref[...], res_ref[...]
-    image = (3.0 * scale_ref[0]) * product + noise_ref[0] * direction
+    image = factor_ref[0:1, 0:1] * product + factor_ref[1:2, 0:1] * direction
     image_ref[...] = image
     rows = lax.broadcasted_iota(jnp.int32, (8, 128), 0)
     lanes = lax.broadcasted_iota(jnp.int32, (8, 128), 1)
@@ -242,7 +242,12 @@
         return jax.ShapeDtypeStruct(shape, dtype)
 
     def partner(group, col):
-        return (group + (col if col else groups // 2)) % groups
+        z, x = divmod(group, 4)
+        if col == 1:
+            dz, dx = ((0, 2), (2, 0))[(z // 2 + x // 2 + 1) % 2]
+        else:
+            dz, dx = {4: (-2, -2), 5: (0, 1), 6: (-1, -2), 7: (1, 0), 2: (-2, -1), 3: (-1, -1), 0: (-1, 1)}[col]
+        return (z + dz) % 4 * 4 + (x + dx) % 4
 
     sent = pl.pallas_call(
         send_kernel,
@@ -263,14 +268,16 @@
         (partner(group, col) * per_group + col, group * per_group + col) for group, col in places
     ]
     other = lax.ppermute(own, both, fetch)
-    left, own_right, own_dir = call(
+    left, own_right, own_dir, factors = call(
         own_kernel,
         [
             array(group_pts, depth, dtype=bf16),
             array(depth, group_pts, dtype=bf16),
             array(16, group_pts, dtype=bf16),
+            array(8, 128),
         ],
-        own,
+        outputscale, noise, own,
+        smem=2,
     )
     place = jnp.stack([lax.axis_index("row"), lax.axis_index("col")]).astype(jnp.int32)
     tile = pltpu.VMEM((width, width), bf16)
@@ -293,8 +300,7 @@
     image, sums = call(
         image_kernel,
         [array(8, width), array(groups * per_group, 128)],
-        outputscale, noise, parts, direction, residual,
-        smem=2,
+        factors, parts, direction, residual,
     )
     sums = lax.all_to_all(sums, both, split_axis=0, concat_axis=0, tiled=True)
     return tuple(

time: 101 us -> 96.9 us (0.959)
  blocking collectives: 29.9 us -> 41.5 us
  waiting for transfers between devices: 16.3 us -> 8.13 us
  starting transfers between devices: 10.4 us -> 5.29 us
  Pallas kernels: 42 us -> 39.4 us
    all_to_all x0 -> x1, blocking collectives: none -> 13.4 us  [shards(): parts = lax.all_to_all(total, 'col', split_axis=0, concat_axis=0)]
    ppermute x1, waiting for transfers between devices: 9.19 us -> 4.79 us  [shards(): back = lax.ppermute(other_out, both, [(to, source) for source, to in fetch])]
    all_to_all x1 -> x0, starting transfers between devices: 4.38 us -> none  [shards(): parts = lax.all_to_all(total, 'col', split_axis=0, concat_axis=0)]
    all_to_all x1 -> x0, waiting for transfers between devices: 3.98 us -> none  [shards(): parts = lax.all_to_all(total, 'col', split_axis=0, concat_axis=0)]
    ppermute x1, starting transfers between devices: 5.95 us -> 2.74 us  [shards(): other = lax.ppermute(own, both, fetch)]
    pallas_call x5, Pallas kernels: 40.4 us -> 37.9 us  [call(): pl.pallas_call(kernel, out_shape=outs, in_specs=[scalars if i < smem else...]
    ppermute x1, starting transfers between devices: 0.07 us -> 2.55 us  [shards(): back = lax.ppermute(other_out, both, [(to, source) for source, to in fetch])]
    all_to_all x1, blocking collectives: 17.4 us -> 15.6 us  [shards(): sums = lax.all_to_all(sums, both, split_axis=0, concat_axis=0, tiled=True)]
  transfers between devices with their start and end apart: 3 -> 2, of which waited for: 3 -> 2; matrix products, arithmetic and copies ran while one was open for 0% -> 0% of each run, Pallas kernels for 0% -> 0%
where the time goes in v3:
time: 96.9 us; the launch traced here: 96.4 us
  blocking collectives  41.5 us (43%)
  Pallas kernels  39.4 us (41%)
  waiting for transfers between devices  8.13 us (8%)
  starting transfers between devices  5.29 us (5%)
  between operations  1.99 us (2%)
    pallas_call x5, Pallas kernels, call(): pl.pallas_call(kernel, out_shape=outs, in_specs=[scalars if i < smem else...  37.9 us
    all_to_all x1, blocking collectives, shards(): sums = lax.all_to_all(sums, both, split_axis=0, concat_axis=0, tiled=True)  15.6 us
    all_to_all x1, blocking collectives, shards(): parts = lax.all_to_all(total, 'col', split_axis=0, concat_axis=0)  13.4 us
    all_to_all x1, blocking collectives, shards(): own = lax.all_to_all(sent, 'col', split_axis=0, concat_axis=0)  12.5 us
    ppermute x1, waiting for transfers between devices, shards(): back = lax.ppermute(other_out, both, [(to, source) for source, to in fetch])  4.79 us
    ppermute x1, waiting for transfers between devices, shards(): other = lax.ppermute(own, both, fetch)  3.34 us
    ppermute x1, starting transfers between devices, shards(): other = lax.ppermute(own, both, fetch)  2.74 us
    ppermute x1, starting transfers between devices, shards(): back = lax.ppermute(other_out, both, [(to, source) for source, to in fetch])  2.55 us
  transfers between devices with their start and end apart: 2, of which 2 were waited for; matrix products, arithmetic and copies ran while one was open for 0% of the time, Pallas kernels for 0%

profile of v3, /device:TPU:1, one launch (start us, length us, event | category | flops | bytes accessed | tf_op | source)
XLA Modules:
  0.0 96.4 jit_solution(16733854057756876352)
XLA Ops:
  0.6 1.5 %shard_map.94 = f32[8,16,512]{2,1,0:T(8,128)} custom-call(f32[8,512]{1,0:T(8,128)} %pts_hbm.1, f32[8]{0:T(128)} %len_hbm.1, f32[8,512]{1,0:T(8,128)} %dir_ref.3), custom_call_target="tpu_custom_call" | custom-call | tf_op jit(solution)/shard_map/pallas_call | solution.py:252
  2.2 12.5 %all_to_all.21.own_ref = f32[8,16,512]{2,1,0:T(8,128)S(1)} all-to-all(f32[8,16,512]{2,1,0:T(8,128)} %shard_map.94), channel_id=1, replica_groups=mesh['row'=16,'col'=8] {'col'}, dimensions={0} | all-to-all | bytes 524288 | tf_op jit(solution)/shard_map/all_to_all | solution.py:265
  14.7 2.7 %collective-permute-start = (f32[8,16,512]{2,1,0:T(8,128)S(1)}, f32[8,16,512]{2,1,0:T(8,128)S(1)}, u32[]{:S(2)}, u32[]{:S(2)}) collective-permute-start(f32[8,16,512]{2,1,0:T(8,128)S(1)} %all_to_all.21.own_ref), channel_id=1, source_target_pairs={{104,0},{65,1},{90,2},{123,3},{84,4},{13,5},{118,6},{39,7},{112,8}... | collective-permute-start | bytes 786440 | tf_op jit(solution)/shard_map/ppermute | solution.py:270
  18.7 0.1 pad_add_fusion.place_ref
  18.8 0.4 shard_map.95
  19.2 3.3 %collective-permute-done.other_ref = f32[8,16,512]{2,1,0:T(8,128)S(1)} collective-permute-done((f32[8,16,512]{2,1,0:T(8,128)S(1)}, f32[8,16,512]{2,1,0:T(8,128)S(1)}, u32[]{:S(2)}, u32[]{:S(2)}) %collective-permute-start) | collective-permute-done | bytes 262176 | tf_op jit(solution)/shard_map/ppermute | solution.py:270
  22.5 36.6 %shard_map.96 = (f32[8,8,512]{2,1,0:T(8,128)S(1)}, f32[8,8,512]{2,1,0:T(8,128)S(1)}) custom-call(s32[2]{0:T(128)S(1)} %pad_add_fusion.place_ref, bf16[4096,64]{1,0:T(8,128)(2,1)S(1)} %get-tuple-element.12.left_ref, bf16[64,4096]{1,0:T(8,128)(2,1)S(1)} %get-tuple-element.13.own_right_ref, bf16[16,4096]{1,0:T(8,128)(2,1)S(1)} %get-tuple-element.14.own_dir_ref, ...), custom_call_target="tpu_custom_call" | custom-call | tf_op jit(solution)/shard_map/pallas_call | solution.py:229
  59.1 2.5 %collective-permute-start.1 = (f32[8,8,512]{2,1,0:T(8,128)S(1)}, f32[8,8,512]{2,1,0:T(8,128)S(1)}, u32[]{:S(2)}, u32[]{:S(2)}) collective-permute-start(f32[8,8,512]{2,1,0:T(8,128)S(1)} %get-tuple-element.16), channel_id=1, source_target_pairs={{0,104},{1,65},{2,90},{3,123},{4,84},{5,13},{6,118},{7,39},{8,112}... | collective-permute-start | bytes 393224 | tf_op jit(solution)/shard_map/ppermute | solution.py:297
  61.7 4.8 %collective-permute-done.1.two_ref = f32[8,8,512]{2,1,0:T(8,128)S(1)} collective-permute-done((f32[8,8,512]{2,1,0:T(8,128)S(1)}, f32[8,8,512]{2,1,0:T(8,128)S(1)}, u32[]{:S(2)}, u32[]{:S(2)}) %collective-permute-start.1) | collective-permute-done | bytes 131104 | tf_op jit(solution)/shard_map/ppermute | solution.py:297
  66.5 0.0 copy-start
  66.5 0.0 copy-start.1
  66.5 13.4 %all_to_all.22.parts_ref = f32[8,8,512]{2,1,0:T(8,128)S(1)} all-to-all(f32[8,8,512]{2,1,0:T(8,128)S(1)} %shard_map.97), channel_id=1, replica_groups=mesh['row'=16,'col'=8] {'col'}, dimensions={0} | all-to-all | bytes 262144 | tf_op jit(solution)/shard_map/all_to_all | solution.py:299
  79.9 0.0 copy-done
  79.9 0.0 copy-done.1
  79.9 0.1 shard_map.98
  80.1 0.0 copy-start.2
  80.1 15.6 %all_to_all.23 = f32[128,1,128]{2,1,0:T(1,128)S(1)} all-to-all(f32[128,1,128]{2,1,0:T(1,128)S(1)} %bitcast.7), channel_id=1, replica_groups=mesh['row'=16,'col'=8] {'row','col'}, dimensions={0} | all-to-all | bytes 131072 | tf_op jit(solution)/shard_map/all_to_all | solution.py:305
  95.7 0.0 copy-done.2
  95.7 0.7 shard_map.99
  (1 shorter events, 0.0 us)
Async XLA Ops:
  14.7 7.9 %collective-permute-start = (f32[8,16,512]{2,1,0:T(8,128)S(1)}, f32[8,16,512]{2,1,0:T(8,128)S(1)}, u32[]{:S(2)}, u32[]{:S(2)}) collective-permute-start(f32[8,16,512]{2,1,0:T(8,128)S(1)} %all_to_all.21.own_ref), channel_id=1, source_target_pairs={{104,0},{65,1},{90,2},{123,3},{84,4},{13,5},{118,6},{39,7},{112,8}... | collective-permute-start | bytes 786440 | tf_op jit(solution)/shard_map/ppermute | solution.py:270
  59.1 7.3 %collective-permute-start.1 = (f32[8,8,512]{2,1,0:T(8,128)S(1)}, f32[8,8,512]{2,1,0:T(8,128)S(1)}, u32[]{:S(2)}, u32[]{:S(2)}) collective-permute-start(f32[8,8,512]{2,1,0:T(8,128)S(1)} %get-tuple-element.16), channel_id=1, source_target_pairs={{0,104},{1,65},{2,90},{3,123},{4,84},{5,13},{6,118},{7,39},{8,112}... | collective-permute-start | bytes 393224 | tf_op jit(solution)/shard_map/ppermute | solution.py:297
  66.5 13.4 %copy-start = (f32[8,512]{1,0:T(8,128)S(1)}, f32[8,512]{1,0:T(8,128)}, u32[]{:S(2)}) copy-start(f32[8,512]{1,0:T(8,128)} %dir_ref.3) | copy-start | bytes 49156
  66.5 13.4 %copy-start.1 = (f32[8,512]{1,0:T(8,128)S(1)}, f32[8,512]{1,0:T(8,128)}, u32[]{:S(2)}) copy-start(f32[8,512]{1,0:T(8,128)} %res_ref.3) | copy-start | bytes 49156
  80.1 15.7 %copy-start.2 = (f32[8,512]{1,0:T(8,128)S(1)}, f32[8,512]{1,0:T(8,128)}, u32[]{:S(2)}) copy-start(f32[8,512]{1,0:T(8,128)} %sol_ref.1) | copy-start | bytes 49156

commit v4 on v3

--- a/solution.py
+++ b/solution.py
@@ -8,6 +8,7 @@
 width = 512
 per_group = 8
 groups = 16
+early = 2
 group_pts = width * per_group
 depth = 64
 chunk = 128
@@ -101,14 +102,14 @@
     return ((dist + 1.0 / 3.0) + radius) * decay
 
 
-def tile_of(step, group, col):
+def tile_of(step, group, col, blocks, alone_from, inner_from):
     halved = col == half_col
-    pairs = jnp.where(halved, 32, 64)
-    pair_row = jnp.where(halved, step // 4, step // 8)
-    pair_col = 8 + jnp.where(halved, 2 * (step % 4) + (pair_row + group // 8) % 2, step % 8)
-    inner = step - pairs + jnp.where(halved, 7, jnp.where(col > half_col, col - 1, col))
-    alone = inner >= 28
-    row = jnp.where(alone, inner - 28, inner % 8)
+    pairs = jnp.where(halved, 4 * blocks, 8 * blocks)
+    pair_row = step % 8
+    pair_col = 8 + jnp.where(halved, 2 * (step // 8) + (pair_row + group // 8) % 2, step // 8)
+    inner = step - pairs + jnp.where(halved, inner_from, jnp.where(col > half_col, col - 1, col))
+    alone = inner >= alone_from
+    row = jnp.where(alone, inner - alone_from, inner % 8)
     column = jnp.where(alone, row, (row + 1 + inner // 8) % 8)
     mixed = step < pairs
     return (
@@ -118,18 +119,28 @@
     )
 
 
-def pair_kernel(place_ref, left_ref, own_right_ref, own_dir_ref, other_ref, own_out, other_out,
-                right_ref, dir_ref, acc_ref, top_even, low_even, top_odd, low_odd):
+def pair_kernel(blocks, inner_from, turns, place_ref, left_ref, own_right_ref, own_dir_ref, other_ref, *refs):
+    before_ref = None
+    if len(refs) == 11:
+        before_ref, first_ref, *refs = refs
+    own_out, other_out, right_ref, dir_ref, acc_ref, top_even, low_even, top_odd, low_odd = refs
     group, col = place_ref[0], place_ref[1]
+    halved = col == half_col
     right_ref[:, :group_pts] = own_right_ref[...]
     dir_ref[:, :group_pts] = own_dir_ref[...]
-    for at in range(per_group):
+    for at in range(blocks):
         right_and_dir(other_ref[at, 0:8, :], other_ref[at, 8:16, :], right_ref, dir_ref, per_group + at)
     acc_ref[...] = jnp.zeros_like(acc_ref)
+    if before_ref is not None:
+        for at in range(per_group):
+            acc_ref[0:8, at * width : (at + 1) * width] = before_ref[at]
+
+    def place_of(step):
+        row, column, weight = tile_of(step, group, col, blocks, 28, inner_from)
+        return pl.multiple_of(row * width, width), pl.multiple_of(column * width, width), weight
 
     def evaluate(step, top, low):
-        row, column, _ = tile_of(step, group, col)
-        row, column = pl.multiple_of(row * width, width), pl.multiple_of(column * width, width)
+        row, column, _ = place_of(step)
 
         def part(at):
             rows = slice(at * chunk, (at + 1) * chunk)
@@ -143,8 +154,7 @@
         return [lambda at=at: part(at) for at in range(width // chunk)]
 
     def multiply(step, top, low):
-        row, column, weight = tile_of(step, group, col)
-        row, column = pl.multiple_of(row * width, width), pl.multiple_of(column * width, width)
+        row, column, weight = place_of(step)
 
         def to_column(tile):
             acc_ref[:, pl.ds(column, width)] += weight * dot(
@@ -174,20 +184,34 @@
         run(evaluate(step + 2, top_even, low_even), multiply(step + 1, top_odd, low_odd))
         return carry
 
-    lax.fori_loop(0, 28, turn, 0, unroll=4)
-    halved = col == half_col
-
-    def last_turns(index, carry):
-        return turn(2 * index + 29, turn(2 * index + 28, carry))
-
-    lax.fori_loop(0, jnp.where(halved, 1, 2), last_turns, 0)
-    for part in multiply(jnp.where(halved, 60, 64), top_even, low_even):
-        part()
+    turns(halved, turn, evaluate, multiply, run, (top_even, low_even), (top_odd, low_odd))
     for at in range(per_group):
         cols = slice(at * width, (at + 1) * width)
         own_out[at] = acc_ref[0:8, cols] + acc_ref[8:16, cols]
+    if before_ref is not None:
+        other_out[0:early] = first_ref[...]
+    for at in range(blocks):
         cols = slice(group_pts + at * width, group_pts + (at + 1) * width)
-        other_out[at] = acc_ref[0:8, cols] + acc_ref[8:16, cols]
+        other_out[at + other_out.shape[0] - blocks] = acc_ref[0:8, cols] + acc_ref[8:16, cols]
+
+
+def first_turns(halved, turn, evaluate, multiply, run, even, odd):
+    lax.fori_loop(0, 6, turn, 0, unroll=3)
+    turn(6, 0)
+    run(evaluate(15, *odd), multiply(14, *even))
+    for part in multiply(15, *odd):
+        part()
+
+
+def later_turns(halved, turn, evaluate, multiply, run, even, odd):
+    lax.fori_loop(0, 20, turn, 0, unroll=4)
+
+    def last_turns(index, carry):
+        return turn(2 * index + 21, turn(2 * index + 20, carry))
+
+    lax.fori_loop(0, jnp.where(halved, 1, 2), last_turns, 0)
+    for part in multiply(jnp.where(halved, 44, 48), *even):
+        part()
 
 
 def image_kernel(factor_ref, parts_ref, dir_ref, res_ref, image_ref, sums_ref):
@@ -267,7 +291,8 @@
     fetch = [
         (partner(group, col) * per_group + col, group * per_group + col) for group, col in places
     ]
-    other = lax.ppermute(own, both, fetch)
+    other_first = lax.ppermute(own[:early], both, fetch)
+    other_later = lax.ppermute(own[early:], both, fetch)
     left, own_right, own_dir, factors = call(
         own_kernel,
         [
@@ -281,21 +306,36 @@
     )
     place = jnp.stack([lax.axis_index("row"), lax.axis_index("col")]).astype(jnp.int32)
     tile = pltpu.VMEM((width, width), bf16)
-    own_out, other_out = call(
-        pair_kernel,
-        [array(per_group, 8, width), array(per_group, 8, width)],
-        place, left, own_right, own_dir, other,
-        smem=1,
-        scratch=[
-            pltpu.VMEM((depth, 2 * group_pts), bf16),
-            pltpu.VMEM((16, 2 * group_pts), bf16),
-            pltpu.VMEM((16, 2 * group_pts), f32),
-            tile, tile, tile, tile,
-        ],
-        limit=32 << 20,
-    )
-    back = lax.ppermute(other_out, both, [(to, source) for source, to in fetch])
-    total = call(add_kernel, array(per_group, 8, width), own_out, back)
+
+    def pair_call(blocks, inner_from, turns, tiles, *args):
+        def body(*refs):
+            pair_kernel(blocks, inner_from, turns, *refs)
+
+        pairs = tiles * width * width
+        pts = group_pts + blocks * width
+        return call(
+            body,
+            [array(per_group, 8, width), array(per_group if len(args) > 1 else blocks, 8, width)],
+            place, left, own_right, own_dir, *args,
+            smem=1,
+            scratch=[
+                pltpu.VMEM((depth, pts), bf16),
+                pltpu.VMEM((16, pts), bf16),
+                pltpu.VMEM((16, pts), f32),
+                tile, tile, tile, tile,
+            ],
+            limit=32 << 20,
+            cost=pl.CostEstimate(
+                flops=256 * pairs, transcendentals=2 * pairs, bytes_accessed=1 << 21
+            ),
+        )
+
+    own_first, out_first = pair_call(early, 7, first_turns, 16, other_first)
+    own_all, out_all = pair_call(
+        per_group - early, 15, later_turns, 49, other_later, own_first, out_first
+    )
+    back = lax.ppermute(out_all, both, [(to, source) for source, to in fetch])
+    total = call(add_kernel, array(per_group, 8, width), own_all, back)
     parts = lax.all_to_all(total, "col", split_axis=0, concat_axis=0)
     image, sums = call(
         image_kernel,

time: 96.9 us -> 95.9 us (0.990)
  blocking collectives: 41.5 us -> 29.8 us
  starting transfers between devices: 5.29 us -> 13.8 us
  Pallas kernels: 39.4 us -> 40.6 us
  waiting for transfers between devices: 8.13 us -> 9.23 us
    all_to_all x1 -> x0, blocking collectives: 12.5 us -> none  [shards(): own = lax.all_to_all(sent, 'col', split_axis=0, concat_axis=0)]
    all_to_all x0 -> x1, starting transfers between devices: none -> 5.98 us  [shards(): own = lax.all_to_all(sent, 'col', split_axis=0, concat_axis=0)]
    all_to_all x0 -> x1, waiting for transfers between devices: none -> 5.2 us  [shards(): own = lax.all_to_all(sent, 'col', split_axis=0, concat_axis=0)]
    ppermute x2 -> x3, waiting for transfers between devices: 8.13 us -> 4.03 us  [the longest x1 4.02 us: shards(): back = lax.ppermute(out_all, both, [(to, source) for source, to in fetch])]
    ppermute x2 -> x3, starting transfers between devices: 5.29 us -> 7.78 us  [the longest x1 3.67 us: shards(): other_later = lax.ppermute(own[early:], both, fetch)]
    all_to_all x1, blocking collectives: 15.6 us -> 17.4 us  [shards(): sums = lax.all_to_all(sums, both, split_axis=0, concat_axis=0, tiled=True)]
    pallas_call x5 -> x6, Pallas kernels: 37.9 us -> 39 us  [call(): pl.pallas_call(kernel, out_shape=outs, in_specs=[scalars if i < smem else...]
  transfers between devices with their start and end apart: 2 -> 4, of which waited for: 2 -> 2; matrix products, arithmetic and copies ran while one was open for 0% -> 0% of each run, Pallas kernels for 0% -> 11%
where the time goes in v4:
time: 95.9 us; the launch traced here: 95.5 us
  Pallas kernels  40.6 us (42%)
  blocking collectives  29.8 us (31%)
  starting transfers between devices  13.8 us (14%)
  waiting for transfers between devices  9.23 us (10%)
  between operations  2.01 us (2%)
    pallas_call x6, Pallas kernels, call(): pl.pallas_call(kernel, out_shape=outs, in_specs=[scalars if i < smem else...  39 us
    all_to_all x1, blocking collectives, shards(): sums = lax.all_to_all(sums, both, split_axis=0, concat_axis=0, tiled=True)  17.4 us
    all_to_all x1, blocking collectives, shards(): parts = lax.all_to_all(total, 'col', split_axis=0, concat_axis=0)  12.4 us
    all_to_all x1, starting transfers between devices, shards(): own = lax.all_to_all(sent, 'col', split_axis=0, concat_axis=0)  5.98 us
    all_to_all x1, waiting for transfers between devices, shards(): own = lax.all_to_all(sent, 'col', split_axis=0, concat_axis=0)  5.2 us
    ppermute x1, waiting for transfers between devices, shards(): back = lax.ppermute(out_all, both, [(to, source) for source, to in fetch])  4.02 us
    ppermute x1, starting transfers between devices, shards(): other_later = lax.ppermute(own[early:], both, fetch)  3.67 us
    ppermute x1, starting transfers between devices, shards(): other_first = lax.ppermute(own[:early], both, fetch)  2.74 us
  transfers between devices with their start and end apart: 4, of which 2 were waited for; matrix products, arithmetic and copies ran while one was open for 0% of the time, Pallas kernels for 11%

profile of v4, /device:TPU:1, one launch (start us, length us, event | category | flops | bytes accessed | tf_op | source)
XLA Modules:
  0.0 95.5 jit_solution(8975231417239518376)
XLA Ops:
  0.6 1.6 %shard_map.94 = f32[8,16,512]{2,1,0:T(8,128)} custom-call(f32[8,512]{1,0:T(8,128)} %pts_hbm.1, f32[8]{0:T(128)} %len_hbm.1, f32[8,512]{1,0:T(8,128)} %dir_ref.3), custom_call_target="tpu_custom_call" | custom-call | tf_op jit(solution)/shard_map/pallas_call | solution.py:276
  2.2 6.0 %all-to-all-start = ((f32[8,16,512]{2,1,0:T(8,128)}), f32[8,16,512]{2,1,0:T(8,128)S(1)}, u32[]{:S(2)}, u32[]{:S(2)}) async-start(f32[8,16,512]{2,1,0:T(8,128)} %shard_map.94), calls=%async_computation | async-start | bytes 524288 | tf_op jit(solution)/shard_map/all_to_all | solution.py:289
  9.5 5.2 %all-to-all-done.own_ref = f32[8,16,512]{2,1,0:T(8,128)S(1)} async-done(((f32[8,16,512]{2,1,0:T(8,128)}), f32[8,16,512]{2,1,0:T(8,128)S(1)}, u32[]{:S(2)}, u32[]{:S(2)}) %all-to-all-start) | async-done | bytes 262176 | tf_op jit(solution)/shard_map/all_to_all | solution.py:289
  14.7 2.7 %collective-permute-start.1 = (f32[2,16,512]{2,1,0:T(8,128)S(1)}, f32[2,16,512]{2,1,0:T(8,128)S(1)}, u32[]{:S(2)}, u32[]{:S(2)}) collective-permute-start(f32[2,16,512]{2,1,0:T(8,128)S(1)} %slice.9), channel_id=1, source_target_pairs={{104,0},{65,1},{90,2},{123,3},{84,4},{13,5},{118,6},{39,7},{112,8}... | collective-permute-start | bytes 196616 | tf_op jit(solution)/shard_map/ppermute | solution.py:294
  17.4 3.7 %collective-permute-start = (f32[6,16,512]{2,1,0:T(8,128)S(1)}, f32[6,16,512]{2,1,0:T(8,128)S(1)}, u32[]{:S(2)}, u32[]{:S(2)}) collective-permute-start(f32[6,16,512]{2,1,0:T(8,128)S(1)} %slice.8), channel_id=1, source_target_pairs={{104,0},{65,1},{90,2},{123,3},{84,4},{13,5},{118,6},{39,7},{112,8}... | collective-permute-start | bytes 589832 | tf_op jit(solution)/shard_map/ppermute | solution.py:295
  21.1 0.1 pad_add_fusion.refs_0_
  21.2 0.4 shard_map.95
  21.6 0.0 collective-permute-done.1.refs_4_
  21.6 9.9 %shard_map.96 = (f32[8,8,512]{2,1,0:T(8,128)S(1)}, f32[2,8,512]{2,1,0:T(8,128)S(1)}) custom-call(s32[2]{0:T(128)S(1)} %pad_add_fusion.refs_0_, bf16[4096,64]{1,0:T(8,128)(2,1)S(1)} %get-tuple-element.14.refs_1_, bf16[64,4096]{1,0:T(8,128)(2,1)S(1)} %get-tuple-element.15.refs_2_, bf16[16,4096]{1,0:T(8,128)(2,1)S(1)} %get-tuple-element.16.refs_3_, ...), custom_call_target="tpu_custom_call" | custom-call | flops 1073741824 | bytes 2097152 | tf_op jit(solution)/shard_map/pallas_call | solution.py:253
  31.5 0.0 collective-permute-done.refs_4_
  31.5 27.9 %shard_map.97 = (f32[8,8,512]{2,1,0:T(8,128)S(1)}, f32[8,8,512]{2,1,0:T(8,128)S(1)}) custom-call(s32[2]{0:T(128)S(1)} %pad_add_fusion.refs_0_, bf16[4096,64]{1,0:T(8,128)(2,1)S(1)} %get-tuple-element.14.refs_1_, bf16[64,4096]{1,0:T(8,128)(2,1)S(1)} %get-tuple-element.15.refs_2_, bf16[16,4096]{1,0:T(8,128)(2,1)S(1)} %get-tuple-element.16.refs_3_, ...), custom_call_target="tpu_custom_call" | custom-call | flops 3288334336 | bytes 2097152 | tf_op jit(solution)/shard_map/pallas_call | solution.py:253
  59.4 1.4 %collective-permute-start.2 = (f32[8,8,512]{2,1,0:T(8,128)S(1)}, f32[8,8,512]{2,1,0:T(8,128)S(1)}, u32[]{:S(2)}, u32[]{:S(2)}) collective-permute-start(f32[8,8,512]{2,1,0:T(8,128)S(1)} %get-tuple-element.20), channel_id=1, source_target_pairs={{0,104},{1,65},{2,90},{3,123},{4,84},{5,13},{6,118},{7,39},{8,112}... | collective-permute-start | bytes 393224 | tf_op jit(solution)/shard_map/ppermute | solution.py:337
  60.7 4.0 %collective-permute-done.2.two_ref = f32[8,8,512]{2,1,0:T(8,128)S(1)} collective-permute-done((f32[8,8,512]{2,1,0:T(8,128)S(1)}, f32[8,8,512]{2,1,0:T(8,128)S(1)}, u32[]{:S(2)}, u32[]{:S(2)}) %collective-permute-start.2) | collective-permute-done | bytes 131104 | tf_op jit(solution)/shard_map/ppermute | solution.py:337
  64.8 0.0 copy-start
  64.8 0.0 copy-start.1
  64.8 12.4 %all_to_all.21.parts_ref = f32[8,8,512]{2,1,0:T(8,128)S(1)} all-to-all(f32[8,8,512]{2,1,0:T(8,128)S(1)} %shard_map.98), channel_id=1, replica_groups=mesh['row'=16,'col'=8] {'col'}, dimensions={0} | all-to-all | bytes 262144 | tf_op jit(solution)/shard_map/all_to_all | solution.py:339
  77.2 0.0 copy-done
  77.2 0.0 copy-done.1
  77.2 0.1 shard_map.99
  77.4 0.0 copy-start.2
  77.4 17.4 %all_to_all.22 = f32[128,1,128]{2,1,0:T(1,128)S(1)} all-to-all(f32[128,1,128]{2,1,0:T(1,128)S(1)} %bitcast.7), channel_id=1, replica_groups=mesh['row'=16,'col'=8] {'row','col'}, dimensions={0} | all-to-all | bytes 131072 | tf_op jit(solution)/shard_map/all_to_all | solution.py:345
  94.8 0.0 copy-done.2
  94.8 0.7 shard_map.100
  (3 shorter events, 0.0 us)
Async XLA Ops:
  2.2 12.5 %all-to-all-start = ((f32[8,16,512]{2,1,0:T(8,128)}), f32[8,16,512]{2,1,0:T(8,128)S(1)}, u32[]{:S(2)}, u32[]{:S(2)}) async-start(f32[8,16,512]{2,1,0:T(8,128)} %shard_map.94), calls=%async_computation | async-start | bytes 524288 | tf_op jit(solution)/shard_map/all_to_all | solution.py:289
  14.7 6.9 %collective-permute-start.1 = (f32[2,16,512]{2,1,0:T(8,128)S(1)}, f32[2,16,512]{2,1,0:T(8,128)S(1)}, u32[]{:S(2)}, u32[]{:S(2)}) collective-permute-start(f32[2,16,512]{2,1,0:T(8,128)S(1)} %slice.9), channel_id=1, source_target_pairs={{104,0},{65,1},{90,2},{123,3},{84,4},{13,5},{118,6},{39,7},{112,8}... | collective-permute-start | bytes 196616 | tf_op jit(solution)/shard_map/ppermute | solution.py:294
  17.4 14.1 %collective-permute-start = (f32[6,16,512]{2,1,0:T(8,128)S(1)}, f32[6,16,512]{2,1,0:T(8,128)S(1)}, u32[]{:S(2)}, u32[]{:S(2)}) collective-permute-start(f32[6,16,512]{2,1,0:T(8,128)S(1)} %slice.8), channel_id=1, source_target_pairs={{104,0},{65,1},{90,2},{123,3},{84,4},{13,5},{118,6},{39,7},{112,8}... | collective-permute-start | bytes 589832 | tf_op jit(solution)/shard_map/ppermute | solution.py:295
  59.4 5.4 %collective-permute-start.2 = (f32[8,8,512]{2,1,0:T(8,128)S(1)}, f32[8,8,512]{2,1,0:T(8,128)S(1)}, u32[]{:S(2)}, u32[]{:S(2)}) collective-permute-start(f32[8,8,512]{2,1,0:T(8,128)S(1)} %get-tuple-element.20), channel_id=1, source_target_pairs={{0,104},{1,65},{2,90},{3,123},{4,84},{5,13},{6,118},{7,39},{8,112}... | collective-permute-start | bytes 393224 | tf_op jit(solution)/shard_map/ppermute | solution.py:337
  64.8 12.5 %copy-start = (f32[8,512]{1,0:T(8,128)S(1)}, f32[8,512]{1,0:T(8,128)}, u32[]{:S(2)}) copy-start(f32[8,512]{1,0:T(8,128)} %dir_ref.3) | copy-start | bytes 49156
  64.8 12.4 %copy-start.1 = (f32[8,512]{1,0:T(8,128)S(1)}, f32[8,512]{1,0:T(8,128)}, u32[]{:S(2)}) copy-start(f32[8,512]{1,0:T(8,128)} %res_ref.3) | copy-start | bytes 49156
  77.4 17.4 %copy-start.2 = (f32[8,512]{1,0:T(8,128)S(1)}, f32[8,512]{1,0:T(8,128)}, u32[]{:S(2)}) copy-start(f32[8,512]{1,0:T(8,128)} %sol_ref.1) | copy-start | bytes 49156

commit v5 on v4

--- a/solution.py
+++ b/solution.py
@@ -121,9 +121,11 @@
 
 def pair_kernel(blocks, inner_from, turns, place_ref, left_ref, own_right_ref, own_dir_ref, other_ref, *refs):
     before_ref = None
-    if len(refs) == 11:
-        before_ref, first_ref, *refs = refs
-    own_out, other_out, right_ref, dir_ref, acc_ref, top_even, low_even, top_odd, low_odd = refs
+    if len(refs) == 13:
+        before_ref, first_ref, top_in, low_in, *refs = refs
+        own_out, other_out, right_ref, dir_ref, acc_ref, top_odd, low_odd, top_even, low_even = refs
+    else:
+        own_out, other_out, top_even, low_even, right_ref, dir_ref, acc_ref, top_odd, low_odd = refs
     group, col = place_ref[0], place_ref[1]
     halved = col == half_col
     right_ref[:, :group_pts] = own_right_ref[...]
@@ -136,7 +138,14 @@
             acc_ref[0:8, at * width : (at + 1) * width] = before_ref[at]
 
     def place_of(step):
-        row, column, weight = tile_of(step, group, col, blocks, 28, inner_from)
+        if before_ref is None:
+            row, column, weight = tile_of(step, group, col, blocks, 28, inner_from)
+        else:
+            handed = tile_of(16, group, col, early, 28, 7)
+            later = tile_of(step - 1, group, col, blocks, 28, inner_from)
+            row, column, weight = (
+                jnp.where(step == 0, one, two) for one, two in zip(handed, later, strict=True)
+            )
         return pl.multiple_of(row * width, width), pl.multiple_of(column * width, width), weight
 
     def evaluate(step, top, low):
@@ -175,8 +184,12 @@
             one()
             two()
 
-    for part in evaluate(0, top_even, low_even):
-        part()
+    if before_ref is None:
+        for part in evaluate(0, top_even, low_even):
+            part()
+    else:
+        top_even[...] = top_in[...]
+        low_even[...] = low_in[...]
 
     def turn(index, carry):
         step = 2 * index
@@ -196,11 +209,7 @@
 
 
 def first_turns(halved, turn, evaluate, multiply, run, even, odd):
-    lax.fori_loop(0, 6, turn, 0, unroll=3)
-    turn(6, 0)
-    run(evaluate(15, *odd), multiply(14, *even))
-    for part in multiply(15, *odd):
-        part()
+    lax.fori_loop(0, 8, turn, 0, unroll=4)
 
 
 def later_turns(halved, turn, evaluate, multiply, run, even, odd):
@@ -315,14 +324,15 @@
         pts = group_pts + blocks * width
         return call(
             body,
-            [array(per_group, 8, width), array(per_group if len(args) > 1 else blocks, 8, width)],
+            [array(per_group, 8, width), array(per_group if len(args) > 1 else blocks, 8, width)]
+            + ([] if len(args) > 1 else [array(width, width, dtype=bf16)] * 2),
             place, left, own_right, own_dir, *args,
             smem=1,
             scratch=[
                 pltpu.VMEM((depth, pts), bf16),
                 pltpu.VMEM((16, pts), bf16),
                 pltpu.VMEM((16, pts), f32),
-                tile, tile, tile, tile,
+                *([tile] * (4 if len(args) > 1 else 2)),
             ],
             limit=32 << 20,
             cost=pl.CostEstimate(
@@ -330,9 +340,9 @@
             ),
         )
 
-    own_first, out_first = pair_call(early, 7, first_turns, 16, other_first)
+    own_first, out_first, top, low = pair_call(early, 7, first_turns, 16, other_first)
     own_all, out_all = pair_call(
-        per_group - early, 15, later_turns, 49, other_later, own_first, out_first
+        per_group - early, 16, later_turns, 49, other_later, own_first, out_first, top, low
     )
     back = lax.ppermute(out_all, both, [(to, source) for source, to in fetch])
     total = call(add_kernel, array(per_group, 8, width), own_all, back)

time: 95.9 us -> 95.8 us (level)
  no operation moved by 1% of the time
where the time goes in v5:
time: 95.8 us; the launch traced here: 95.4 us
  Pallas kernels  40.5 us (42%)
  blocking collectives  29.8 us (31%)
  starting transfers between devices  13.8 us (14%)
  waiting for transfers between devices  9.24 us (10%)
  between operations  2.01 us (2%)
    pallas_call x6, Pallas kernels, call(): pl.pallas_call(kernel, out_shape=outs, in_specs=[scalars if i < smem else...  38.9 us
    all_to_all x1, blocking collectives, shards(): sums = lax.all_to_all(sums, both, split_axis=0, concat_axis=0, tiled=True)  17.4 us
    all_to_all x1, blocking collectives, shards(): parts = lax.all_to_all(total, 'col', split_axis=0, concat_axis=0)  12.4 us
    all_to_all x1, starting transfers between devices, shards(): own = lax.all_to_all(sent, 'col', split_axis=0, concat_axis=0)  5.98 us
    all_to_all x1, waiting for transfers between devices, shards(): own = lax.all_to_all(sent, 'col', split_axis=0, concat_axis=0)  5.2 us
    ppermute x1, waiting for transfers between devices, shards(): back = lax.ppermute(out_all, both, [(to, source) for source, to in fetch])  4.03 us
    ppermute x1, starting transfers between devices, shards(): other_later = lax.ppermute(own[early:], both, fetch)  3.67 us
    ppermute x1, starting transfers between devices, shards(): other_first = lax.ppermute(own[:early], both, fetch)  2.74 us
  transfers between devices with their start and end apart: 4, of which 2 were waited for; matrix products, arithmetic and copies ran while one was open for 0% of the time, Pallas kernels for 11%

profile of v5, /device:TPU:1, one launch (start us, length us, event | category | flops | bytes accessed | tf_op | source)
XLA Modules:
  0.0 95.4 jit_solution(501790351132939093)
XLA Ops:
  0.6 1.6 %shard_map.94 = f32[8,16,512]{2,1,0:T(8,128)} custom-call(f32[8,512]{1,0:T(8,128)} %pts_hbm.1, f32[8]{0:T(128)} %len_hbm.1, f32[8,512]{1,0:T(8,128)} %dir_ref.3), custom_call_target="tpu_custom_call" | custom-call | tf_op jit(solution)/shard_map/pallas_call | solution.py:285
  2.2 6.0 %all-to-all-start = ((f32[8,16,512]{2,1,0:T(8,128)}), f32[8,16,512]{2,1,0:T(8,128)S(1)}, u32[]{:S(2)}, u32[]{:S(2)}) async-start(f32[8,16,512]{2,1,0:T(8,128)} %shard_map.94), calls=%async_computation | async-start | bytes 524288 | tf_op jit(solution)/shard_map/all_to_all | solution.py:298
  9.5 5.2 %all-to-all-done.own_ref = f32[8,16,512]{2,1,0:T(8,128)S(1)} async-done(((f32[8,16,512]{2,1,0:T(8,128)}), f32[8,16,512]{2,1,0:T(8,128)S(1)}, u32[]{:S(2)}, u32[]{:S(2)}) %all-to-all-start) | async-done | bytes 262176 | tf_op jit(solution)/shard_map/all_to_all | solution.py:298
  14.7 2.7 %collective-permute-start.1 = (f32[2,16,512]{2,1,0:T(8,128)S(1)}, f32[2,16,512]{2,1,0:T(8,128)S(1)}, u32[]{:S(2)}, u32[]{:S(2)}) collective-permute-start(f32[2,16,512]{2,1,0:T(8,128)S(1)} %slice.9), channel_id=1, source_target_pairs={{104,0},{65,1},{90,2},{123,3},{84,4},{13,5},{118,6},{39,7},{112,8}... | collective-permute-start | bytes 196616 | tf_op jit(solution)/shard_map/ppermute | solution.py:303
  17.4 3.7 %collective-permute-start = (f32[6,16,512]{2,1,0:T(8,128)S(1)}, f32[6,16,512]{2,1,0:T(8,128)S(1)}, u32[]{:S(2)}, u32[]{:S(2)}) collective-permute-start(f32[6,16,512]{2,1,0:T(8,128)S(1)} %slice.8), channel_id=1, source_target_pairs={{104,0},{65,1},{90,2},{123,3},{84,4},{13,5},{118,6},{39,7},{112,8}... | collective-permute-start | bytes 589832 | tf_op jit(solution)/shard_map/ppermute | solution.py:304
  21.1 0.1 pad_add_fusion.refs_0_
  21.2 0.4 shard_map.95
  21.6 0.0 collective-permute-done.1.refs_4_
  21.6 10.4 %shard_map.96 = (f32[8,8,512]{2,1,0:T(8,128)S(1)}, f32[2,8,512]{2,1,0:T(8,128)S(1)}, bf16[512,512]{1,0:T(8,128)(2,1)S(1)}, bf16[512,512]{1,0:T(8,128)(2,1)S(1)}) custom-call(s32[2]{0:T(128)S(1)} %pad_add_fusion.refs_0_, bf16[4096,64]{1,0:T(8,128)(2,1)S(1)} %get-tuple-element.16.refs_1_, bf16[64,4096]{1,0:T(8,128)(2,1)S(1)} %get-tuple-element.17.refs_2_, ...), custom_call_target="tpu_custom_call" | custom-call | flops 1073741824 | bytes 2097152 | tf_op jit(solution)/shard_map/pallas_call | solution.py:262
  32.0 0.0 collective-permute-done.refs_4_
  32.0 27.3 %shard_map.97 = (f32[8,8,512]{2,1,0:T(8,128)S(1)}, f32[8,8,512]{2,1,0:T(8,128)S(1)}) custom-call(s32[2]{0:T(128)S(1)} %pad_add_fusion.refs_0_, bf16[4096,64]{1,0:T(8,128)(2,1)S(1)} %get-tuple-element.16.refs_1_, bf16[64,4096]{1,0:T(8,128)(2,1)S(1)} %get-tuple-element.17.refs_2_, bf16[16,4096]{1,0:T(8,128)(2,1)S(1)} %get-tuple-element.18.refs_3_, ...), custom_call_target="tpu_custom_call" | custom-call | flops 3288334336 | bytes 2097152 | tf_op jit(solution)/shard_map/pallas_call | solution.py:262
  59.3 1.4 %collective-permute-start.2 = (f32[8,8,512]{2,1,0:T(8,128)S(1)}, f32[8,8,512]{2,1,0:T(8,128)S(1)}, u32[]{:S(2)}, u32[]{:S(2)}) collective-permute-start(f32[8,8,512]{2,1,0:T(8,128)S(1)} %get-tuple-element.24), channel_id=1, source_target_pairs={{0,104},{1,65},{2,90},{3,123},{4,84},{5,13},{6,118},{7,39},{8,112}... | collective-permute-start | bytes 393224 | tf_op jit(solution)/shard_map/ppermute | solution.py:347
  60.6 4.0 %collective-permute-done.2.two_ref = f32[8,8,512]{2,1,0:T(8,128)S(1)} collective-permute-done((f32[8,8,512]{2,1,0:T(8,128)S(1)}, f32[8,8,512]{2,1,0:T(8,128)S(1)}, u32[]{:S(2)}, u32[]{:S(2)}) %collective-permute-start.2) | collective-permute-done | bytes 131104 | tf_op jit(solution)/shard_map/ppermute | solution.py:347
  64.7 0.0 copy-start
  64.7 0.0 copy-start.1
  64.7 12.4 %all_to_all.21.parts_ref = f32[8,8,512]{2,1,0:T(8,128)S(1)} all-to-all(f32[8,8,512]{2,1,0:T(8,128)S(1)} %shard_map.98), channel_id=1, replica_groups=mesh['row'=16,'col'=8] {'col'}, dimensions={0} | all-to-all | bytes 262144 | tf_op jit(solution)/shard_map/all_to_all | solution.py:349
  77.1 0.0 copy-done
  77.1 0.0 copy-done.1
  77.1 0.1 shard_map.99
  77.3 0.0 copy-start.2
  77.3 17.4 %all_to_all.22 = f32[128,1,128]{2,1,0:T(1,128)S(1)} all-to-all(f32[128,1,128]{2,1,0:T(1,128)S(1)} %bitcast.7), channel_id=1, replica_groups=mesh['row'=16,'col'=8] {'row','col'}, dimensions={0} | all-to-all | bytes 131072 | tf_op jit(solution)/shard_map/all_to_all | solution.py:355
  94.7 0.0 copy-done.2
  94.7 0.7 shard_map.100
  (3 shorter events, 0.0 us)
Async XLA Ops:
  2.2 12.5 %all-to-all-start = ((f32[8,16,512]{2,1,0:T(8,128)}), f32[8,16,512]{2,1,0:T(8,128)S(1)}, u32[]{:S(2)}, u32[]{:S(2)}) async-start(f32[8,16,512]{2,1,0:T(8,128)} %shard_map.94), calls=%async_computation | async-start | bytes 524288 | tf_op jit(solution)/shard_map/all_to_all | solution.py:298
  14.7 6.9 %collective-permute-start.1 = (f32[2,16,512]{2,1,0:T(8,128)S(1)}, f32[2,16,512]{2,1,0:T(8,128)S(1)}, u32[]{:S(2)}, u32[]{:S(2)}) collective-permute-start(f32[2,16,512]{2,1,0:T(8,128)S(1)} %slice.9), channel_id=1, source_target_pairs={{104,0},{65,1},{90,2},{123,3},{84,4},{13,5},{118,6},{39,7},{112,8}... | collective-permute-start | bytes 196616 | tf_op jit(solution)/shard_map/ppermute | solution.py:303
  17.4 14.5 %collective-permute-start = (f32[6,16,512]{2,1,0:T(8,128)S(1)}, f32[6,16,512]{2,1,0:T(8,128)S(1)}, u32[]{:S(2)}, u32[]{:S(2)}) collective-permute-start(f32[6,16,512]{2,1,0:T(8,128)S(1)} %slice.8), channel_id=1, source_target_pairs={{104,0},{65,1},{90,2},{123,3},{84,4},{13,5},{118,6},{39,7},{112,8}... | collective-permute-start | bytes 589832 | tf_op jit(solution)/shard_map/ppermute | solution.py:304
  59.3 5.4 %collective-permute-start.2 = (f32[8,8,512]{2,1,0:T(8,128)S(1)}, f32[8,8,512]{2,1,0:T(8,128)S(1)}, u32[]{:S(2)}, u32[]{:S(2)}) collective-permute-start(f32[8,8,512]{2,1,0:T(8,128)S(1)} %get-tuple-element.24), channel_id=1, source_target_pairs={{0,104},{1,65},{2,90},{3,123},{4,84},{5,13},{6,118},{7,39},{8,112}... | collective-permute-start | bytes 393224 | tf_op jit(solution)/shard_map/ppermute | solution.py:347
  64.7 12.5 %copy-start = (f32[8,512]{1,0:T(8,128)S(1)}, f32[8,512]{1,0:T(8,128)}, u32[]{:S(2)}) copy-start(f32[8,512]{1,0:T(8,128)} %dir_ref.3) | copy-start | bytes 49156
  64.7 12.4 %copy-start.1 = (f32[8,512]{1,0:T(8,128)S(1)}, f32[8,512]{1,0:T(8,128)}, u32[]{:S(2)}) copy-start(f32[8,512]{1,0:T(8,128)} %res_ref.3) | copy-start | bytes 49156
  77.3 17.4 %copy-start.2 = (f32[8,512]{1,0:T(8,128)S(1)}, f32[8,512]{1,0:T(8,128)}, u32[]{:S(2)}) copy-start(f32[8,512]{1,0:T(8,128)} %sol_ref.1) | copy-start | bytes 49156

commit v6 on v5

--- a/solution.py
+++ b/solution.py
@@ -213,12 +213,14 @@
 
 
 def later_turns(halved, turn, evaluate, multiply, run, even, odd):
-    lax.fori_loop(0, 20, turn, 0, unroll=4)
-
-    def last_turns(index, carry):
-        return turn(2 * index + 21, turn(2 * index + 20, carry))
-
-    lax.fori_loop(0, jnp.where(halved, 1, 2), last_turns, 0)
+    def two_turns(index, carry):
+        return turn(2 * index + 1, turn(2 * index, carry))
+
+    def four_turns(index, carry):
+        return two_turns(2 * index + 1, two_turns(2 * index, carry))
+
+    lax.fori_loop(0, jnp.where(halved, 5, 6), four_turns, 0)
+    lax.fori_loop(10, jnp.where(halved, 11, 10), two_turns, 0)
     for part in multiply(jnp.where(halved, 44, 48), *even):
         part()
 
@@ -276,10 +278,10 @@
 
     def partner(group, col):
         z, x = divmod(group, 4)
-        if col == 1:
+        if col == 5:
             dz, dx = ((0, 2), (2, 0))[(z // 2 + x // 2 + 1) % 2]
         else:
-            dz, dx = {4: (-2, -2), 5: (0, 1), 6: (-1, -2), 7: (1, 0), 2: (-2, -1), 3: (-1, -1), 0: (-1, 1)}[col]
+            dz, dx = {0: (0, 1), 1: (1, 0), 2: (-2, -1), 3: (1, 1), 4: (2, 2), 6: (-1, -2), 7: (1, -1)}[col]
         return (z + dz) % 4 * 4 + (x + dx) % 4
 
     sent = pl.pallas_call(

time: 95.8 us -> 95.8 us (level)
  starting transfers between devices: 13.8 us -> 10.7 us
  waiting for transfers between devices: 9.24 us -> 10.8 us
  blocking collectives: 29.8 us -> 31.3 us
    ppermute x1, starting transfers between devices: 3.67 us -> 0.19 us  [shards(): other_later = lax.ppermute(own[early:], both, fetch)]
    all_to_all x1, blocking collectives: 12.4 us -> 14.6 us  [shards(): parts = lax.all_to_all(total, 'col', split_axis=0, concat_axis=0)]
    ppermute x1, starting transfers between devices: 2.74 us -> 3.76 us  [shards(): other_first = lax.ppermute(own[:early], both, fetch)]
  transfers between devices with their start and end apart: 4 -> 4, of which waited for: 2 -> 3; matrix products, arithmetic and copies ran while one was open for 0% -> 0% of each run, Pallas kernels for 11% -> 11%
where the time goes in v6:
time: 95.8 us; the launch traced here: 95.3 us
  Pallas kernels  40.4 us (42%)
  blocking collectives  31.3 us (33%)
  waiting for transfers between devices  10.8 us (11%)
  starting transfers between devices  10.7 us (11%)
  between operations  2.01 us (2%)
    pallas_call x6, Pallas kernels, call(): pl.pallas_call(kernel, out_shape=outs, in_specs=[scalars if i < smem else...  38.9 us
    all_to_all x1, blocking collectives, shards(): sums = lax.all_to_all(sums, both, split_axis=0, concat_axis=0, tiled=True)  16.8 us
    all_to_all x1, blocking collectives, shards(): parts = lax.all_to_all(total, 'col', split_axis=0, concat_axis=0)  14.6 us
    all_to_all x1, starting transfers between devices, shards(): own = lax.all_to_all(sent, 'col', split_axis=0, concat_axis=0)  5.98 us
    all_to_all x1, waiting for transfers between devices, shards(): own = lax.all_to_all(sent, 'col', split_axis=0, concat_axis=0)  5.2 us
    ppermute x1, waiting for transfers between devices, shards(): back = lax.ppermute(out_all, both, [(to, source) for source, to in fetch])  4.94 us
    ppermute x1, starting transfers between devices, shards(): other_first = lax.ppermute(own[:early], both, fetch)  3.76 us
  transfers between devices with their start and end apart: 4, of which 3 were waited for; matrix products, arithmetic and copies ran while one was open for 0% of the time, Pallas kernels for 11%

profile of v6, /device:TPU:1, one launch (start us, length us, event | category | flops | bytes accessed | tf_op | source)
XLA Modules:
  0.0 95.3 jit_solution(7598934285338499851)
XLA Ops:
  0.6 1.6 %shard_map.94 = f32[8,16,512]{2,1,0:T(8,128)} custom-call(f32[8,512]{1,0:T(8,128)} %pts_hbm.1, f32[8]{0:T(128)} %len_hbm.1, f32[8,512]{1,0:T(8,128)} %dir_ref.3), custom_call_target="tpu_custom_call" | custom-call | tf_op jit(solution)/shard_map/pallas_call | solution.py:287
  2.2 6.0 %all-to-all-start = ((f32[8,16,512]{2,1,0:T(8,128)}), f32[8,16,512]{2,1,0:T(8,128)S(1)}, u32[]{:S(2)}, u32[]{:S(2)}) async-start(f32[8,16,512]{2,1,0:T(8,128)} %shard_map.94), calls=%async_computation | async-start | bytes 524288 | tf_op jit(solution)/shard_map/all_to_all | solution.py:300
  9.5 5.2 %all-to-all-done.own_ref = f32[8,16,512]{2,1,0:T(8,128)S(1)} async-done(((f32[8,16,512]{2,1,0:T(8,128)}), f32[8,16,512]{2,1,0:T(8,128)S(1)}, u32[]{:S(2)}, u32[]{:S(2)}) %all-to-all-start) | async-done | bytes 262176 | tf_op jit(solution)/shard_map/all_to_all | solution.py:300
  14.7 3.8 %collective-permute-start.1 = (f32[2,16,512]{2,1,0:T(8,128)S(1)}, f32[2,16,512]{2,1,0:T(8,128)S(1)}, u32[]{:S(2)}, u32[]{:S(2)}) collective-permute-start(f32[2,16,512]{2,1,0:T(8,128)S(1)} %slice.9), channel_id=1, source_target_pairs={{8,0},{33,1},{90,2},{43,3},{84,4},{69,5},{118,6},{63,7},{16,8},{41... | collective-permute-start | bytes 196616 | tf_op jit(solution)/shard_map/ppermute | solution.py:305
  18.5 0.2 collective-permute-start
  18.6 0.1 pad_add_fusion.refs_0_
  18.7 0.4 shard_map.95
  19.1 0.7 collective-permute-done.1.refs_4_
  19.8 10.4 %shard_map.96 = (f32[8,8,512]{2,1,0:T(8,128)S(1)}, f32[2,8,512]{2,1,0:T(8,128)S(1)}, bf16[512,512]{1,0:T(8,128)(2,1)S(1)}, bf16[512,512]{1,0:T(8,128)(2,1)S(1)}) custom-call(s32[2]{0:T(128)S(1)} %pad_add_fusion.refs_0_, bf16[4096,64]{1,0:T(8,128)(2,1)S(1)} %get-tuple-element.16.refs_1_, bf16[64,4096]{1,0:T(8,128)(2,1)S(1)} %get-tuple-element.17.refs_2_, ...), custom_call_target="tpu_custom_call" | custom-call | flops 1073741824 | bytes 2097152 | tf_op jit(solution)/shard_map/pallas_call | solution.py:264
  30.1 0.0 collective-permute-done.refs_4_
  30.2 27.2 %shard_map.97 = (f32[8,8,512]{2,1,0:T(8,128)S(1)}, f32[8,8,512]{2,1,0:T(8,128)S(1)}) custom-call(s32[2]{0:T(128)S(1)} %pad_add_fusion.refs_0_, bf16[4096,64]{1,0:T(8,128)(2,1)S(1)} %get-tuple-element.16.refs_1_, bf16[64,4096]{1,0:T(8,128)(2,1)S(1)} %get-tuple-element.17.refs_2_, bf16[16,4096]{1,0:T(8,128)(2,1)S(1)} %get-tuple-element.18.refs_3_, ...), custom_call_target="tpu_custom_call" | custom-call | flops 3288334336 | bytes 2097152 | tf_op jit(solution)/shard_map/pallas_call | solution.py:264
  57.4 0.8 collective-permute-start.2
  58.2 4.9 %collective-permute-done.2.two_ref = f32[8,8,512]{2,1,0:T(8,128)S(1)} collective-permute-done((f32[8,8,512]{2,1,0:T(8,128)S(1)}, f32[8,8,512]{2,1,0:T(8,128)S(1)}, u32[]{:S(2)}, u32[]{:S(2)}) %collective-permute-start.2) | collective-permute-done | bytes 131104 | tf_op jit(solution)/shard_map/ppermute | solution.py:349
  63.1 0.0 copy-start
  63.1 0.0 copy-start.1
  63.1 14.6 %all_to_all.21.parts_ref = f32[8,8,512]{2,1,0:T(8,128)S(1)} all-to-all(f32[8,8,512]{2,1,0:T(8,128)S(1)} %shard_map.98), channel_id=1, replica_groups=mesh['row'=16,'col'=8] {'col'}, dimensions={0} | all-to-all | bytes 262144 | tf_op jit(solution)/shard_map/all_to_all | solution.py:351
  77.7 0.0 copy-done
  77.7 0.0 copy-done.1
  77.7 0.1 shard_map.99
  77.9 0.0 copy-start.2
  77.9 16.8 %all_to_all.22 = f32[128,1,128]{2,1,0:T(1,128)S(1)} all-to-all(f32[128,1,128]{2,1,0:T(1,128)S(1)} %bitcast.7), channel_id=1, replica_groups=mesh['row'=16,'col'=8] {'row','col'}, dimensions={0} | all-to-all | bytes 131072 | tf_op jit(solution)/shard_map/all_to_all | solution.py:357
  94.6 0.0 copy-done.2
  94.6 0.7 shard_map.100
  (3 shorter events, 0.0 us)
Async XLA Ops:
  2.2 12.5 %all-to-all-start = ((f32[8,16,512]{2,1,0:T(8,128)}), f32[8,16,512]{2,1,0:T(8,128)S(1)}, u32[]{:S(2)}, u32[]{:S(2)}) async-start(f32[8,16,512]{2,1,0:T(8,128)} %shard_map.94), calls=%async_computation | async-start | bytes 524288 | tf_op jit(solution)/shard_map/all_to_all | solution.py:300
  14.7 5.1 %collective-permute-start.1 = (f32[2,16,512]{2,1,0:T(8,128)S(1)}, f32[2,16,512]{2,1,0:T(8,128)S(1)}, u32[]{:S(2)}, u32[]{:S(2)}) collective-permute-start(f32[2,16,512]{2,1,0:T(8,128)S(1)} %slice.9), channel_id=1, source_target_pairs={{8,0},{33,1},{90,2},{43,3},{84,4},{69,5},{118,6},{63,7},{16,8},{41... | collective-permute-start | bytes 196616 | tf_op jit(solution)/shard_map/ppermute | solution.py:305
  18.5 11.7 %collective-permute-start = (f32[6,16,512]{2,1,0:T(8,128)S(1)}, f32[6,16,512]{2,1,0:T(8,128)S(1)}, u32[]{:S(2)}, u32[]{:S(2)}) collective-permute-start(f32[6,16,512]{2,1,0:T(8,128)S(1)} %slice.8), channel_id=1, source_target_pairs={{8,0},{33,1},{90,2},{43,3},{84,4},{69,5},{118,6},{63,7},{16,8},{41... | collective-permute-start | bytes 589832 | tf_op jit(solution)/shard_map/ppermute | solution.py:306
  57.4 5.7 %collective-permute-start.2 = (f32[8,8,512]{2,1,0:T(8,128)S(1)}, f32[8,8,512]{2,1,0:T(8,128)S(1)}, u32[]{:S(2)}, u32[]{:S(2)}) collective-permute-start(f32[8,8,512]{2,1,0:T(8,128)S(1)} %get-tuple-element.24), channel_id=1, source_target_pairs={{0,8},{1,33},{2,90},{3,43},{4,84},{5,69},{6,118},{7,63},{8,16},{9,... | collective-permute-start | bytes 393224 | tf_op jit(solution)/shard_map/ppermute | solution.py:349
  63.1 14.6 %copy-start = (f32[8,512]{1,0:T(8,128)S(1)}, f32[8,512]{1,0:T(8,128)}, u32[]{:S(2)}) copy-start(f32[8,512]{1,0:T(8,128)} %dir_ref.3) | copy-start | bytes 49156
  63.1 14.6 %copy-start.1 = (f32[8,512]{1,0:T(8,128)S(1)}, f32[8,512]{1,0:T(8,128)}, u32[]{:S(2)}) copy-start(f32[8,512]{1,0:T(8,128)} %res_ref.3) | copy-start | bytes 49156
  77.9 16.8 %copy-start.2 = (f32[8,512]{1,0:T(8,128)S(1)}, f32[8,512]{1,0:T(8,128)}, u32[]{:S(2)}) copy-start(f32[8,512]{1,0:T(8,128)} %sol_ref.1) | copy-start | bytes 49156

commit v7 on v6

--- a/solution.py
+++ b/solution.py
@@ -278,10 +278,10 @@
 
     def partner(group, col):
         z, x = divmod(group, 4)
-        if col == 5:
+        if col == 1:
             dz, dx = ((0, 2), (2, 0))[(z // 2 + x // 2 + 1) % 2]
         else:
-            dz, dx = {0: (0, 1), 1: (1, 0), 2: (-2, -1), 3: (1, 1), 4: (2, 2), 6: (-1, -2), 7: (1, -1)}[col]
+            dz, dx = {4: (-2, -2), 5: (0, 1), 6: (-1, -2), 7: (1, 0), 2: (-2, -1), 3: (-1, -1), 0: (-1, 1)}[col]
         return (z + dz) % 4 * 4 + (x + dx) % 4
 
     sent = pl.pallas_call(

time: 95.8 us -> 95.8 us (level)
  starting transfers between devices: 10.7 us -> 13.8 us
  waiting for transfers between devices: 10.8 us -> 9.22 us
  blocking collectives: 31.3 us -> 29.8 us
    ppermute x1, starting transfers between devices: 0.19 us -> 3.67 us  [shards(): other_later = lax.ppermute(own[early:], both, fetch)]
    all_to_all x1, blocking collectives: 14.6 us -> 12.4 us  [shards(): parts = lax.all_to_all(total, 'col', split_axis=0, concat_axis=0)]
    ppermute x1, starting transfers between devices: 3.76 us -> 2.74 us  [shards(): other_first = lax.ppermute(own[:early], both, fetch)]
  transfers between devices with their start and end apart: 4 -> 4, of which waited for: 3 -> 2; matrix products, arithmetic and copies ran while one was open for 0% -> 0% of each run, Pallas kernels for 11% -> 11%
where the time goes in v7:
time: 95.8 us; the launch traced here: 95.3 us
  Pallas kernels  40.4 us (42%)
  blocking collectives  29.8 us (31%)
  starting transfers between devices  13.8 us (14%)
  waiting for transfers between devices  9.22 us (10%)
  between operations  2.01 us (2%)
    pallas_call x6, Pallas kernels, call(): pl.pallas_call(kernel, out_shape=outs, in_specs=[scalars if i < smem else...  38.9 us
    all_to_all x1, blocking collectives, shards(): sums = lax.all_to_all(sums, both, split_axis=0, concat_axis=0, tiled=True)  17.4 us
    all_to_all x1, blocking collectives, shards(): parts = lax.all_to_all(total, 'col', split_axis=0, concat_axis=0)  12.4 us
    all_to_all x1, starting transfers between devices, shards(): own = lax.all_to_all(sent, 'col', split_axis=0, concat_axis=0)  5.98 us
    all_to_all x1, waiting for transfers between devices, shards(): own = lax.all_to_all(sent, 'col', split_axis=0, concat_axis=0)  5.2 us
    ppermute x1, waiting for transfers between devices, shards(): back = lax.ppermute(out_all, both, [(to, source) for source, to in fetch])  4.01 us
    ppermute x1, starting transfers between devices, shards(): other_later = lax.ppermute(own[early:], both, fetch)  3.67 us
    ppermute x1, starting transfers between devices, shards(): other_first = lax.ppermute(own[:early], both, fetch)  2.74 us
  transfers between devices with their start and end apart: 4, of which 2 were waited for; matrix products, arithmetic and copies ran while one was open for 0% of the time, Pallas kernels for 11%

profile of v7, /device:TPU:1, one launch (start us, length us, event | category | flops | bytes accessed | tf_op | source)
XLA Modules:
  0.0 95.3 jit_solution(14815900203042004550)
XLA Ops:
  0.6 1.6 %shard_map.94 = f32[8,16,512]{2,1,0:T(8,128)} custom-call(f32[8,512]{1,0:T(8,128)} %pts_hbm.1, f32[8]{0:T(128)} %len_hbm.1, f32[8,512]{1,0:T(8,128)} %dir_ref.3), custom_call_target="tpu_custom_call" | custom-call | tf_op jit(solution)/shard_map/pallas_call | solution.py:287
  2.2 6.0 %all-to-all-start = ((f32[8,16,512]{2,1,0:T(8,128)}), f32[8,16,512]{2,1,0:T(8,128)S(1)}, u32[]{:S(2)}, u32[]{:S(2)}) async-start(f32[8,16,512]{2,1,0:T(8,128)} %shard_map.94), calls=%async_computation | async-start | bytes 524288 | tf_op jit(solution)/shard_map/all_to_all | solution.py:300
  9.5 5.2 %all-to-all-done.own_ref = f32[8,16,512]{2,1,0:T(8,128)S(1)} async-done(((f32[8,16,512]{2,1,0:T(8,128)}), f32[8,16,512]{2,1,0:T(8,128)S(1)}, u32[]{:S(2)}, u32[]{:S(2)}) %all-to-all-start) | async-done | bytes 262176 | tf_op jit(solution)/shard_map/all_to_all | solution.py:300
  14.7 2.7 %collective-permute-start.1 = (f32[2,16,512]{2,1,0:T(8,128)S(1)}, f32[2,16,512]{2,1,0:T(8,128)S(1)}, u32[]{:S(2)}, u32[]{:S(2)}) collective-permute-start(f32[2,16,512]{2,1,0:T(8,128)S(1)} %slice.9), channel_id=1, source_target_pairs={{104,0},{65,1},{90,2},{123,3},{84,4},{13,5},{118,6},{39,7},{112,8}... | collective-permute-start | bytes 196616 | tf_op jit(solution)/shard_map/ppermute | solution.py:305
  17.4 3.7 %collective-permute-start = (f32[6,16,512]{2,1,0:T(8,128)S(1)}, f32[6,16,512]{2,1,0:T(8,128)S(1)}, u32[]{:S(2)}, u32[]{:S(2)}) collective-permute-start(f32[6,16,512]{2,1,0:T(8,128)S(1)} %slice.8), channel_id=1, source_target_pairs={{104,0},{65,1},{90,2},{123,3},{84,4},{13,5},{118,6},{39,7},{112,8}... | collective-permute-start | bytes 589832 | tf_op jit(solution)/shard_map/ppermute | solution.py:306
  21.1 0.1 pad_add_fusion.refs_0_
  21.2 0.4 shard_map.95
  21.6 0.0 collective-permute-done.1.refs_4_
  21.6 10.4 %shard_map.96 = (f32[8,8,512]{2,1,0:T(8,128)S(1)}, f32[2,8,512]{2,1,0:T(8,128)S(1)}, bf16[512,512]{1,0:T(8,128)(2,1)S(1)}, bf16[512,512]{1,0:T(8,128)(2,1)S(1)}) custom-call(s32[2]{0:T(128)S(1)} %pad_add_fusion.refs_0_, bf16[4096,64]{1,0:T(8,128)(2,1)S(1)} %get-tuple-element.16.refs_1_, bf16[64,4096]{1,0:T(8,128)(2,1)S(1)} %get-tuple-element.17.refs_2_, ...), custom_call_target="tpu_custom_call" | custom-call | flops 1073741824 | bytes 2097152 | tf_op jit(solution)/shard_map/pallas_call | solution.py:264
  32.0 0.0 collective-permute-done.refs_4_
  32.0 27.2 %shard_map.97 = (f32[8,8,512]{2,1,0:T(8,128)S(1)}, f32[8,8,512]{2,1,0:T(8,128)S(1)}) custom-call(s32[2]{0:T(128)S(1)} %pad_add_fusion.refs_0_, bf16[4096,64]{1,0:T(8,128)(2,1)S(1)} %get-tuple-element.16.refs_1_, bf16[64,4096]{1,0:T(8,128)(2,1)S(1)} %get-tuple-element.17.refs_2_, bf16[16,4096]{1,0:T(8,128)(2,1)S(1)} %get-tuple-element.18.refs_3_, ...), custom_call_target="tpu_custom_call" | custom-call | flops 3288334336 | bytes 2097152 | tf_op jit(solution)/shard_map/pallas_call | solution.py:264
  59.2 1.4 %collective-permute-start.2 = (f32[8,8,512]{2,1,0:T(8,128)S(1)}, f32[8,8,512]{2,1,0:T(8,128)S(1)}, u32[]{:S(2)}, u32[]{:S(2)}) collective-permute-start(f32[8,8,512]{2,1,0:T(8,128)S(1)} %get-tuple-element.24), channel_id=1, source_target_pairs={{0,104},{1,65},{2,90},{3,123},{4,84},{5,13},{6,118},{7,39},{8,112}... | collective-permute-start | bytes 393224 | tf_op jit(solution)/shard_map/ppermute | solution.py:349
  60.6 4.0 %collective-permute-done.2.two_ref = f32[8,8,512]{2,1,0:T(8,128)S(1)} collective-permute-done((f32[8,8,512]{2,1,0:T(8,128)S(1)}, f32[8,8,512]{2,1,0:T(8,128)S(1)}, u32[]{:S(2)}, u32[]{:S(2)}) %collective-permute-start.2) | collective-permute-done | bytes 131104 | tf_op jit(solution)/shard_map/ppermute | solution.py:349
  64.6 0.0 copy-start
  64.6 0.0 copy-start.1
  64.7 12.4 %all_to_all.21.parts_ref = f32[8,8,512]{2,1,0:T(8,128)S(1)} all-to-all(f32[8,8,512]{2,1,0:T(8,128)S(1)} %shard_map.98), channel_id=1, replica_groups=mesh['row'=16,'col'=8] {'col'}, dimensions={0} | all-to-all | bytes 262144 | tf_op jit(solution)/shard_map/all_to_all | solution.py:351
  77.1 0.0 copy-done
  77.1 0.0 copy-done.1
  77.1 0.1 shard_map.99
  77.2 0.0 copy-start.2
  77.2 17.4 %all_to_all.22 = f32[128,1,128]{2,1,0:T(1,128)S(1)} all-to-all(f32[128,1,128]{2,1,0:T(1,128)S(1)} %bitcast.7), channel_id=1, replica_groups=mesh['row'=16,'col'=8] {'row','col'}, dimensions={0} | all-to-all | bytes 131072 | tf_op jit(solution)/shard_map/all_to_all | solution.py:357
  94.6 0.0 copy-done.2
  94.6 0.7 shard_map.100
  (3 shorter events, 0.0 us)
Async XLA Ops:
  2.2 12.5 %all-to-all-start = ((f32[8,16,512]{2,1,0:T(8,128)}), f32[8,16,512]{2,1,0:T(8,128)S(1)}, u32[]{:S(2)}, u32[]{:S(2)}) async-start(f32[8,16,512]{2,1,0:T(8,128)} %shard_map.94), calls=%async_computation | async-start | bytes 524288 | tf_op jit(solution)/shard_map/all_to_all | solution.py:300
  14.7 6.9 %collective-permute-start.1 = (f32[2,16,512]{2,1,0:T(8,128)S(1)}, f32[2,16,512]{2,1,0:T(8,128)S(1)}, u32[]{:S(2)}, u32[]{:S(2)}) collective-permute-start(f32[2,16,512]{2,1,0:T(8,128)S(1)} %slice.9), channel_id=1, source_target_pairs={{104,0},{65,1},{90,2},{123,3},{84,4},{13,5},{118,6},{39,7},{112,8}... | collective-permute-start | bytes 196616 | tf_op jit(solution)/shard_map/ppermute | solution.py:305
  17.4 14.5 %collective-permute-start = (f32[6,16,512]{2,1,0:T(8,128)S(1)}, f32[6,16,512]{2,1,0:T(8,128)S(1)}, u32[]{:S(2)}, u32[]{:S(2)}) collective-permute-start(f32[6,16,512]{2,1,0:T(8,128)S(1)} %slice.8), channel_id=1, source_target_pairs={{104,0},{65,1},{90,2},{123,3},{84,4},{13,5},{118,6},{39,7},{112,8}... | collective-permute-start | bytes 589832 | tf_op jit(solution)/shard_map/ppermute | solution.py:306
  59.2 5.4 %collective-permute-start.2 = (f32[8,8,512]{2,1,0:T(8,128)S(1)}, f32[8,8,512]{2,1,0:T(8,128)S(1)}, u32[]{:S(2)}, u32[]{:S(2)}) collective-permute-start(f32[8,8,512]{2,1,0:T(8,128)S(1)} %get-tuple-element.24), channel_id=1, source_target_pairs={{0,104},{1,65},{2,90},{3,123},{4,84},{5,13},{6,118},{7,39},{8,112}... | collective-permute-start | bytes 393224 | tf_op jit(solution)/shard_map/ppermute | solution.py:349
  64.6 12.4 %copy-start = (f32[8,512]{1,0:T(8,128)S(1)}, f32[8,512]{1,0:T(8,128)}, u32[]{:S(2)}) copy-start(f32[8,512]{1,0:T(8,128)} %dir_ref.3) | copy-start | bytes 49156
  64.6 12.4 %copy-start.1 = (f32[8,512]{1,0:T(8,128)S(1)}, f32[8,512]{1,0:T(8,128)}, u32[]{:S(2)}) copy-start(f32[8,512]{1,0:T(8,128)} %res_ref.3) | copy-start | bytes 49156
  77.2 17.4 %copy-start.2 = (f32[8,512]{1,0:T(8,128)S(1)}, f32[8,512]{1,0:T(8,128)}, u32[]{:S(2)}) copy-start(f32[8,512]{1,0:T(8,128)} %sol_ref.1) | copy-start | bytes 49156
